TPU v7x, 32 devices: a whole 2x2x4 slice. The times are simulated.
32 devices in a mesh: groups: 2 (over x), dp: 8 (over z, y), tensor: 2 (over core).
Axes of the slice: x: 2, y: 2, z: 4, core: 2. Of those that a mesh axis runs over, the one named last changes fastest.
Arguments:
- visual_tokens: bfloat16 [7680, 8192], P(('groups', 'dp'), 'tensor'), parts along dimension 0, may hold values from -800 to 800
- kv_weight: bfloat16 [2, 4096, 2, 512], P('tensor'), may hold values from -0.0625 to 0.0625
- image_lengths: int32 [16, 12], P('groups'), parts along dimension 0, may hold values from 1 to 48, 480 in all within a row
- image_owner: int32 [192], P('groups'), parts along dimension 0, may hold values from 0 to 191, as said below
- cache_lengths: int32 [384], P(('groups', 'dp')), parts along dimension 0, may hold values from 2 to 128
- cache_keys: bfloat16 [384, 128, 512], P(('groups', 'dp'), None, 'tensor'), parts along dimension 0, may hold values from -4.5 to 4.5
- cache_values: bfloat16 [384, 128, 512], P(('groups', 'dp'), None, 'tensor'), parts along dimension 0, may hold values from -4 to 4
- step_queries: bfloat16 [384, 4, 4096], P(('groups', 'dp'), None, 'tensor'), parts along dimension 0, may hold values from -30 to 30
- step_keys: bfloat16 [384, 4, 512], P(('groups', 'dp'), None, 'tensor'), parts along dimension 0, may hold values from -4 to 4
- step_values: bfloat16 [384, 4, 512], P(('groups', 'dp'), None, 'tensor'), parts along dimension 0, may hold values from -4 to 4
Outputs:
- attended: bfloat16 [384, 4, 4096], P(('groups', 'dp'), None, 'tensor'), parts along dimension 0
There are 2 independent parts, one for each index of `groups`. A program takes and returns all parts, laid end to end along the dimension named above; an argument that names none is the same for every part. Nothing has to cross between parts.
Inputs may be any that keep to these rules, and one draw needn't show every extreme that they name: `image_owner`: distinct rows. The images of one source dp index reach at most 3 rows of any one dp index (rows of dp index k: k * 24 to (k + 1) * 24 - 1), and some source reaches 3; some dp index owns 24 screenshots and some own none.
All inputs are finite; a program needn't handle non-finite values.
Results may differ from a plain program's by a relative error of at most 0.0053.
Values may be sent and summed in bfloat16 or wider, within the bound.
No kernel may reach another device: no remote copies, remote signals or barrier semaphores. Data moves between devices by JAX's collectives and lax.ppermute only.
A program may use at most 128 MiB of HBM per device.

v0:
```python
import jax
import jax.numpy as jnp
from jax import lax
from jax.sharding import PartitionSpec as P

D = 8192
HD = 128
STEPS = 4
VMAX = 48


EPSILON = 1e-06


def shards(
    visual_tokens,
    kv_weight,
    image_lengths,
    image_owner,
    cache_lengths,
    cache_keys,
    cache_values,
    step_queries,
    step_keys,
    step_values,
):
    device = lax.axis_index("dp")
    devices = lax.axis_size("dp")
    rows_local = cache_lengths.shape[0]
    images_local = image_lengths.shape[1]
    capacity = -(-rows_local // devices)
    width_local = cache_keys.shape[2]
    kv_local = width_local // HD
    heads_local = step_queries.shape[2] // HD
    group_size = heads_local // kv_local
    weight_half = kv_weight[0]
    features = visual_tokens.astype(jnp.float32)
    squares = lax.psum(jnp.sum(features * features, axis=1), "tensor")
    normed = (features * lax.rsqrt(squares / D + EPSILON)[:, None]).astype(jnp.bfloat16)
    owner_device = (image_owner // rows_local).reshape(devices, images_local)
    same_owner = owner_device[:, :, None] == owner_device[:, None, :]
    order_index = jnp.arange(images_local)
    earlier = order_index[None, :] < order_index[:, None]
    pair_slot = jnp.sum((same_owner & earlier[None, :, :]).astype(jnp.int32), axis=2)
    own_lengths = lax.dynamic_index_in_dim(image_lengths, device, 0, keepdims=False)
    own_owner = lax.dynamic_index_in_dim(owner_device, device, 0, keepdims=False)
    own_slot = lax.dynamic_index_in_dim(pair_slot, device, 0, keepdims=False)
    own_starts = jnp.cumsum(own_lengths) - own_lengths
    target = jnp.arange(devices)[:, None] * capacity + jnp.arange(capacity)[None, :]
    image_key = own_owner * capacity + own_slot
    matches = (target[:, :, None] == image_key[None, None, :]).astype(jnp.int32)
    send_start = jnp.sum(matches * own_starts[None, None, :], axis=2)
    send_length = jnp.sum(matches * own_lengths[None, None, :], axis=2)
    offsets = jnp.arange(VMAX)
    send_valid = offsets[None, None, :] < send_length[:, :, None]
    send_index = jnp.where(send_valid, send_start[:, :, None] + offsets[None, None, :], 0).reshape(
        -1
    )
    send_valid = send_valid.reshape(-1)
    global_rows = device * rows_local + jnp.arange(rows_local)
    row_hits = (image_owner[None, :] == global_rows[:, None]).astype(jnp.int32)
    flat_lengths = image_lengths.reshape(-1)
    image_source = jnp.arange(image_owner.shape[0]) // images_local
    visual_length = jnp.sum(row_hits * flat_lengths[None, :], axis=1)
    pick_slot = jnp.sum(
        row_hits * (image_source * capacity + pair_slot.reshape(-1))[None, :], axis=1
    )
    taken = jnp.take(normed, send_index, axis=0)
    shaped_valid = send_valid.reshape((-1,) + (1,) * (normed.ndim - 1))
    packed = jnp.where(shaped_valid, taken, jnp.zeros_like(taken))
    outgoing = packed.reshape((devices, capacity * VMAX) + normed.shape[1:])
    incoming = lax.all_to_all(outgoing, "dp", split_axis=0, concat_axis=0, tiled=True)
    arrived = jnp.take(
        incoming.reshape(devices * capacity, VMAX, normed.shape[1]), pick_slot, axis=0
    )
    arrived = arrived.reshape(rows_local * VMAX, normed.shape[1])
    partial_value = jnp.einsum(
        "td,dcf->tcf", arrived, weight_half, preferred_element_type=jnp.float32
    )
    summed = lax.psum_scatter(partial_value, "tensor", scatter_dimension=2, tiled=True).astype(
        jnp.bfloat16
    )
    visual_pairs = summed.reshape(rows_local, VMAX, 2, width_local)
    context = cache_keys.shape[1]
    queries = step_queries.reshape(rows_local, STEPS, kv_local, group_size, HD)
    all_keys = jnp.concatenate([cache_keys, visual_pairs[:, :, 0, :], step_keys], axis=1).reshape(
        rows_local, -1, kv_local, HD
    )
    all_values = jnp.concatenate(
        [cache_values, visual_pairs[:, :, 1, :], step_values], axis=1
    ).reshape(rows_local, -1, kv_local, HD)
    scores = jnp.einsum(
        "rsgjd,rpgd->rgjsp", queries, all_keys, preferred_element_type=jnp.float32
    ) * HD ** (-0.5)
    position = jnp.arange(all_keys.shape[1])
    live_cache = position[None, :] < cache_lengths[:, None]
    visual_place = position - context
    live_visual = (visual_place[None, :] >= 0) & (visual_place[None, :] < visual_length[:, None])
    step_place = position - context - VMAX
    live_step = (step_place[None, :] >= 0) & (step_place[None, :] <= jnp.arange(STEPS)[:, None])
    allowed = (live_cache | live_visual)[:, None, None, None, :] | live_step[None, None, None, :, :]
    masked = jnp.where(allowed, scores, -1e30)
    row_peak = jnp.max(masked, axis=-1, keepdims=True)
    weights = jnp.where(allowed, jnp.exp(masked - row_peak), 0.0)
    weights = (weights / jnp.sum(weights, axis=-1, keepdims=True)).astype(jnp.bfloat16)
    mixed = jnp.einsum("rgjsp,rpgd->rsgjd", weights, all_values, preferred_element_type=jnp.float32)
    return mixed.astype(jnp.bfloat16).reshape(rows_local, STEPS, heads_local * HD)


def solution(mesh):
    return jax.shard_map(
        shards,
        mesh=mesh,
        in_specs=(
            P(("groups", "dp"), "tensor"),
            P("tensor", None, None, None),
            P("groups", None),
            P("groups"),
            P(("groups", "dp")),
            P(("groups", "dp"), None, "tensor"),
            P(("groups", "dp"), None, "tensor"),
            P(("groups", "dp"), None, "tensor"),
            P(("groups", "dp"), None, "tensor"),
            P(("groups", "dp"), None, "tensor"),
        ),
        out_specs=P(("groups", "dp"), None, "tensor"),
        check_vma=False,
    )
```

profile of v0, /device:TPU:0, one launch (start us, length us, event | category | flops | bytes accessed | tf_op | source)
XLA Modules:
  0.0 326.2 jit_solution(12309610885520524647)
XLA Ops:
  6.5 0.7 fusion.30
  7.2 0.2 reduce-window.8
  7.4 0.7 bitcast_subtract_fusion
  8.1 0.7 and_select_fusion
  8.8 0.1 eq.44
  8.9 0.1 copy.39
  9.0 0.4 convert_reduce_fusion
  9.3 0.2 add_reduce_fusion
  9.5 0.3 fusion.23
  9.8 0.1 copy.42
  9.8 0.1 copy.43
  9.9 0.1 iota_compare_fusion.1
  10.0 0.1 iota_add_fusion
  10.1 0.1 select_n.109
  10.2 3.0 fusion.3
  13.2 2.6 psum.7
  15.8 5.4 %fusion.4 = bf16[480,4096]{1,0:T(8,128)(2,1)} fusion(bf16[480,4096]{1,0:T(8,128)(2,1)} %param.10, f32[480]{0:T(512)S(1)} %add_rsqrt_fusion), kind=kLoop, calls=%fused_computation.10 | loop fusion | flops 5898240 | bytes 7866240 | tf_op jit(solution)/shard_map/convert_element_type | solution.py:39
  21.2 0.1 add.161
  21.2 0.1 lt.131
  21.3 21.1 %gather_fusion = bf16[1152,4096]{1,0:T(8,128)(2,1)} fusion(bf16[480,4096]{1,0:T(8,128)(2,1)} %fusion.4, s32[2048]{0:T(1024)S(1)} %pad_clamp_fusion), kind=kCustom, calls=%fused_computation | custom fusion | bytes 18878976 | tf_op jit(solution)/shard_map/jit(_take)/gather | solution.py:68
  42.4 8.5 %select_select_fusion = bf16[8,144,4096]{2,1,0:T(8,128)(2,1)} fusion(bf16[8,144,4096]{2,1,0:T(8,128)(2,1)} %bitcast.57, pred[8,144]{1,0:T(8,128)(4,1)S(1)} %compare_and_fusion, pred[8,144]{1,0:T(8,128)(4,1)S(1)} %lt.131), kind=kLoop, calls=%fused_computation.5 | loop fusion | flops 9437184 | bytes 18876672 | tf_op jit(solution)/shard_map/jit(_where)/select_n | solution.py:70
  50.9 7.3 %all-to-all-start = ((bf16[8,144,4096]{2,1,0:T(8,128)(2,1)}), bf16[8,144,4096]{2,1,0:T(8,128)(2,1)}, u32[]{:S(2)}, u32[]{:S(2)}) async-start(bf16[8,144,4096]{2,1,0:T(8,128)(2,1)} %select_select_fusion), calls=%async_computation | async-start | bytes 18874368 | tf_op jit(solution)/shard_map/all_to_all | solution.py:72
  58.2 0.2 reduce-scatter.2.cloned.1.call-start
  58.5 0.1 copy.40
  58.5 0.1 mul.100
  58.6 0.1 reshape.396
  58.7 0.2 fusion.22
  59.0 205.3 %all-to-all-done = bf16[8,144,4096]{2,1,0:T(8,128)(2,1)} async-done(((bf16[8,144,4096]{2,1,0:T(8,128)(2,1)}), bf16[8,144,4096]{2,1,0:T(8,128)(2,1)}, u32[]{:S(2)}, u32[]{:S(2)}) %all-to-all-start) | async-done | bytes 9437216 | tf_op jit(solution)/shard_map/all_to_all | solution.py:72
  264.2 9.6 %gather_fusion.1 = bf16[24,48,4096]{2,1,0:T(8,128)(2,1)} fusion(bf16[24,48,4096]{2,1,0:T(8,128)(2,1)} %bitcast.5, s32[1024]{0:T(1024)S(1)} %pad_clamp_fusion.1), kind=kCustom, calls=%fused_computation.1 | custom fusion | bytes 18874464 | tf_op jit(solution)/shard_map/jit(_take)/gather | solution.py:73
  273.8 8.3 %broadcast_select_fusion = bf16[24,48,4096]{2,1,0:T(8,128)(2,1)} fusion(bf16[24,48,4096]{2,1,0:T(8,128)(2,1)} %gather_fusion.1, pred[24]{0:T(512)(128)(4,1)S(1)} %compare_and_fusion.1), kind=kLoop, calls=%fused_computation.6 | loop fusion | flops 4718592 | bytes 18874392 | tf_op jit(solution)/shard_map/jit(_take)/select_n | solution.py:73
  282.1 15.8 %fusion.1 = f32[1152,2,512]{2,0,1:T(8,128)} fusion(bf16[1152,4096,1]{1,0,2:T(8,128)(2,1)} %bitcast.58, bf16[4096,2,512]{2,1,0:T(2,128)(2,1)} %bitcast.62), kind=kOutput, calls=%fused_computation.7 | convolution fusion | flops 9663676416 | bytes 22544384 | tf_op jit(solution)/shard_map/td,dcf->tcf/dot_general | solution.py:77
  297.8 1.4 copy-done
  299.2 0.9 copy.47
  300.2 1.6 copy.48
  301.8 1.0 reshape.401
  302.8 0.9 copy.38
  303.7 0.9 copy.45
  304.7 0.1 fusion.20
  304.8 4.9 %reduce-scatter.2.cloned.1.call-done = f32[1152,2,256]{2,0,1:T(8,128)} async-done(((f32[1152,2,512]{2,0,1:T(8,128)}), f32[1152,2,256]{2,0,1:T(8,128)}) %reduce-scatter.2.cloned.1.call-update) | async-done | bytes 2359312 | tf_op jit(solution)/shard_map/reduce_scatter | solution.py:80
  309.7 1.8 convert_element_type.26
  311.4 0.1 fusion.35
  311.5 0.1 concatenate.25
  311.7 0.1 copy.49
  311.8 0.1 concatenate.21
  311.9 0.1 copy.46
  312.0 4.2 %fusion.36 = (f32[24,2,8,4]{2,3,1,0:T(4,128)S(1)}, f32[24,2,8,4,180]{4,2,3,1,0:T(8,128)}) fusion(pred[24,4,180]{2,1,0:T(4,128)(4,1)S(1)} %broadcast_or_fusion, bf16[24,4,2,128]{3,1,2,0:T(4,128)(2,1)S(1)} %bitcast.63, bf16[24,48,2,128]{3,1,2,0:T(8,128)(2,1)S(1)} %copy.49, bf16[24,128,2,128]{3,1,2,0:T(8,128)(2,1)} %copy.48, ...), kind=kOutput, calls=%fused_computation.82 | convolution fusion | flops 78796976 | bytes 3734400 | tf_op jit(solution)/shard_map/sub | solution.py:104
  316.3 2.2 fusion.17
  318.5 0.8 reshape.422
  (34 shorter events, 0.3 us)
Async XLA Ops:
  50.9 7.6 %copy-start.3 = (s32[8,12]{1,0:T(8,128)S(1)}, s32[8,12]{1,0:T(8,128)}, u32[]{:S(2)}) copy-start(s32[8,12]{1,0:T(8,128)} %param.12) | copy-start | bytes 1156
  50.9 7.8 %copy-start.5 = (s32[96]{0:T(128)S(1)}, s32[96]{0:T(128)}, u32[]{:S(2)}) copy-start(s32[96]{0:T(128)} %param.13) | copy-start | bytes 1156
  50.9 213.3 %all-to-all-start = ((bf16[8,144,4096]{2,1,0:T(8,128)(2,1)}), bf16[8,144,4096]{2,1,0:T(8,128)(2,1)}, u32[]{:S(2)}, u32[]{:S(2)}) async-start(bf16[8,144,4096]{2,1,0:T(8,128)(2,1)} %select_select_fusion), calls=%async_computation | async-start | bytes 18874368 | tf_op jit(solution)/shard_map/all_to_all | solution.py:72
  58.2 251.4 %reduce-scatter.2.cloned.1.call-start = ((), (), s32[]{:S(2)}) async-start(), calls=%async_computation.2 | async-start | bytes 7077888 | tf_op jit(solution)/shard_map/reduce_scatter | solution.py:80
  297.8 1.4 copy-start
  297.8 4.0 %copy-start.2 = (bf16[24,4,2048]{2,1,0:T(4,128)(2,1)S(1)}, bf16[24,4,2048]{2,1,0:T(4,128)(2,1)}, u32[]{:S(2)}) copy-start(bf16[24,4,2048]{2,1,0:T(4,128)(2,1)} %param.17) | copy-start | bytes 1179652
  300.1 2.7 copy-start.1
  300.1 4.5 %copy-start.4 = (s32[24]{0:T(128)S(1)}, s32[24]{0:T(128)}, u32[]{:S(2)}) copy-start(s32[24]{0:T(128)} %param.14) | copy-start | bytes 292
  304.8 7.2 %copy-start.6 = (bf16[24,4,256]{2,1,0:T(4,128)(2,1)S(1)}, bf16[24,4,256]{2,1,0:T(4,128)(2,1)}, u32[]{:S(2)}) copy-start(bf16[24,4,256]{2,1,0:T(4,128)(2,1)} %param.18) | copy-start | bytes 147460
  312.0 4.3 %copy-start.7 = (bf16[24,4,256]{2,1,0:T(4,128)(2,1)S(1)}, bf16[24,4,256]{2,1,0:T(4,128)(2,1)}, u32[]{:S(2)}) copy-start(bf16[24,4,256]{2,1,0:T(4,128)(2,1)} %param.19) | copy-start | bytes 147460
Sparse Core Ops, SparseCore 0:
  298.0 11.6 reduce-scatter.1
where the time goes:
time: 327 us; the launch traced here: 326 us
  waiting for transfers between devices  210 us (64%)
  local copies, waits for them, and re-layouts  40.3 us (12%)
  other arithmetic  29.9 us (9%)
  matrix products  22.2 us (7%)
  between operations  13.7 us (4%)
  starting transfers between devices  7.51 us (2%)
    all_to_all x1, waiting for transfers between devices, shards(): lax.all_to_all(outgoing, 'dp', split_axis=0, concat_axis=0, tiled=True)  205 us
    gather x1, local copies, waits for them, and re-layouts, shards(): taken = jnp.take(normed, send_index, axis=0)  21.1 us
    dot_general x1, matrix products, shards(): jnp.einsum('td,dcf->tcf', arrived, weight_half, preferred_element_type=jn...  15.8 us
    gather x1, local copies, waits for them, and re-layouts, shards(): jnp.take(incoming.reshape(devices * capacity, VMAX, normed.shape[1]), pic...  9.56 us
    select_n x1, other arithmetic, shards(): packed = jnp.where(shaped_valid, taken, jnp.zeros_like(taken))  8.53 us
    select_n x2, other arithmetic, shards(): jnp.take(incoming.reshape(devices * capacity, VMAX, normed.shape[1]), pic...  8.31 us
    all_to_all x1, starting transfers between devices, shards(): lax.all_to_all(outgoing, 'dp', split_axis=0, concat_axis=0, tiled=True)  7.3 us
  transfers between devices with their start and end apart: 2, of which 2 were waited for; matrix products, arithmetic and copies ran while one was open for 2% of the time, Pallas kernels for 0%

commit v1 on v0

v1 whole, which is shorter than its diff:
```python
import jax
import jax.numpy as jnp
from jax import lax
from jax.experimental import pallas as pl
from jax.experimental.pallas import tpu as pltpu
from jax.sharding import PartitionSpec as P

D = 8192
HD = 128
STEPS = 4
VMAX = 48
EPSILON = 1e-06
LANES = 128
FLOOR = -1e30
VMEM_BYTES = 40 << 20


def dot_t(a, b):
    return lax.dot_general(a, b, (((1,), (1,)), ((), ())), preferred_element_type=jnp.float32)


def dot(a, b):
    return jnp.dot(a, b, preferred_element_type=jnp.float32)


def pack_queries(image_owner, step_queries, devices, capacity):
    rows = step_queries.shape[0]
    images = image_owner.shape[0] // devices
    slots = devices * capacity

    def kernel(owner, queries, packed, slot_of_row, row_of_slot, sems):
        base = lax.axis_index("dp") * rows
        for r in range(rows):
            slot_of_row[r] = -1
        copies = []
        for s in range(devices):
            for k in range(capacity):
                row_of_slot[s * capacity + k] = 0
            rank = jnp.int32(0)
            for i in range(images):
                row = owner[s * images + i] - base
                local = jnp.logical_and(row >= 0, row < rows)
                slot = s * capacity + rank
                row_of_slot[jnp.where(local, slot, slots)] = row
                slot_of_row[jnp.where(local, row, rows)] = slot
                rank = rank + local.astype(jnp.int32)
            for k in range(capacity):
                slot = s * capacity + k
                copy = pltpu.make_async_copy(
                    queries.at[row_of_slot[slot]], packed.at[slot], sems.at[slot]
                )
                copy.start()
                copies.append(copy)
        for copy in copies:
            copy.wait()

    return pl.pallas_call(
        kernel,
        in_specs=[
            pl.BlockSpec(memory_space=pltpu.SMEM),
            pl.BlockSpec(memory_space=pl.ANY),
        ],
        out_specs=[
            pl.BlockSpec(memory_space=pl.ANY),
            pl.BlockSpec(memory_space=pltpu.SMEM),
        ],
        out_shape=[
            jax.ShapeDtypeStruct((slots,) + step_queries.shape[1:], step_queries.dtype),
            jax.ShapeDtypeStruct((rows + 1,), jnp.int32),
        ],
        scratch_shapes=[
            pltpu.SMEM((slots + 1,), jnp.int32),
            pltpu.SemaphoreType.DMA((slots,)),
        ],
        name="pack_queries",
    )(image_owner, step_queries)


def project(tokens, weight, half, with_squares):
    count, depth = tokens.shape
    width = weight.shape[2] // 2
    chunk = 512
    columns = 2 * width + (LANES if with_squares else 0)

    def kernel(half_ref, token_ref, weight_ref, out_ref):
        total = jnp.zeros((count, 2 * width), jnp.float32)
        squares = jnp.zeros((count, LANES), jnp.float32)
        for at in range(0, depth, chunk):
            x = token_ref[:, at : at + chunk]
            w = jnp.swapaxes(weight_ref[at : at + chunk], 0, 1)
            total += dot(x, jnp.concatenate([w[0], w[1]], axis=1))
            if with_squares:
                for lane in range(0, chunk, LANES):
                    wide = x[:, lane : lane + LANES].astype(jnp.float32)
                    squares += wide * wide
        out_ref[:, : 2 * width] = total
        if with_squares:
            out_ref[:, 2 * width :] = jnp.broadcast_to(
                jnp.sum(squares, axis=1, keepdims=True), (count, LANES)
            )

    return pl.pallas_call(
        kernel,
        grid_spec=pltpu.PrefetchScalarGridSpec(
            num_scalar_prefetch=1,
            grid=(1,),
            in_specs=[
                pl.BlockSpec((count, depth), lambda i, half_ref: (0, 0)),
                pl.BlockSpec((depth, 2, width), lambda i, half_ref: (0, 0, half_ref[0])),
            ],
            out_specs=pl.BlockSpec((count, columns), lambda i, half_ref: (0, 0)),
        ),
        out_shape=jax.ShapeDtypeStruct((count, columns), jnp.float32),
        compiler_params=pltpu.CompilerParams(vmem_limit_bytes=VMEM_BYTES),
        cost_estimate=pl.CostEstimate(
            flops=4 * count * depth * width,
            bytes_accessed=2 * depth * (count + 2 * width),
            transcendentals=0,
        ),
        name="project_partner" if with_squares else "project_own",
    )(half.reshape(1), tokens, weight)


def stack_heads(read, store, heads):
    for j in range(heads):
        store(j * STEPS, read(j).astype(jnp.float32))


def cached_attention(queries, cache_keys, cache_values, step_keys, step_values, lengths):
    rows, context, width = cache_keys.shape
    kv_local = width // HD
    heads = queries.shape[2] // HD
    group = heads // kv_local
    stacked = group * STEPS
    block = 8 if rows % 8 == 0 else 1
    scale = HD**-0.5

    def kernel(length_ref, q_ref, k_ref, v_ref, sk_ref, sv_ref, out_ref, log_ref, q_s, sk_s, sv_s):
        first = pl.program_id(0) * block
        for r in range(block):
            for g in range(kv_local):
                sk_s[g, r * STEPS : (r + 1) * STEPS, :] = sk_ref[
                    r, :, g * HD : (g + 1) * HD
                ].astype(jnp.float32)
                sv_s[g, r * STEPS : (r + 1) * STEPS, :] = sv_ref[
                    r, :, g * HD : (g + 1) * HD
                ].astype(jnp.float32)
                for j in range(group):
                    h = g * group + j
                    at = r * stacked + j * STEPS
                    q_s[g, at : at + STEPS, :] = q_ref[r, :, h * HD : (h + 1) * HD].astype(
                        jnp.float32
                    )
        lane = lax.broadcasted_iota(jnp.int32, (STEPS, LANES), 1)
        logs = [jnp.zeros((STEPS, LANES), jnp.float32) for _ in range(block)]
        for g in range(kv_local):
            q = q_s[g].astype(jnp.bfloat16)
            steps = dot_t(q, sk_s[g].astype(jnp.bfloat16)) * scale
            at_row = lax.broadcasted_iota(jnp.int32, steps.shape, 0)
            at_key = lax.broadcasted_iota(jnp.int32, steps.shape, 1)
            own = (at_row // stacked == at_key // STEPS) & (at_key % STEPS <= at_row % STEPS)
            steps = jnp.where(own, steps, FLOOR)
            step_peak = jnp.max(steps, axis=1, keepdims=True)
            scores = []
            position = lax.broadcasted_iota(jnp.int32, (stacked, context), 1)
            for r in range(block):
                part = dot_t(q[r * stacked : (r + 1) * stacked], k_ref[r, :, g * HD : (g + 1) * HD])
                scores.append(jnp.where(position < length_ref[first + r], part * scale, FLOOR))
            cached = jnp.concatenate(scores, axis=0)
            peak = jnp.maximum(jnp.max(cached, axis=1, keepdims=True), step_peak)
            cached = jnp.exp(cached - peak)
            steps = jnp.where(own, jnp.exp(steps - peak), 0.0)
            total = jnp.sum(cached, axis=1, keepdims=True) + jnp.sum(steps, axis=1, keepdims=True)
            cached = cached.astype(jnp.bfloat16)
            mixed = dot(steps.astype(jnp.bfloat16), sv_s[g].astype(jnp.bfloat16))
            inverse = 1.0 / total
            log = jnp.broadcast_to(peak + jnp.log(total), (block * stacked, LANES))
            for r in range(block):
                span = slice(r * stacked, (r + 1) * stacked)
                part = dot(cached[span], v_ref[r, :, g * HD : (g + 1) * HD])
                part = (part + mixed[span]) * inverse[span]
                for j in range(group):
                    h = g * group + j
                    head = slice(j * STEPS, (j + 1) * STEPS)
                    out_ref[r, :, h * HD : (h + 1) * HD] = part[head]
                    at = r * stacked + j * STEPS
                    logs[r] = jnp.where(lane == h, log[at : at + STEPS], logs[r])
        for r in range(block):
            log_ref[r] = logs[r]

    def spec(array):
        return pl.BlockSpec((block,) + array.shape[1:], lambda i, length_ref: (i, 0, 0))

    return pl.pallas_call(
        kernel,
        grid_spec=pltpu.PrefetchScalarGridSpec(
            num_scalar_prefetch=1,
            grid=(rows // block,),
            in_specs=[
                spec(queries),
                spec(cache_keys),
                spec(cache_values),
                spec(step_keys),
                spec(step_values),
            ],
            out_specs=[
                spec(queries),
                pl.BlockSpec((block, STEPS, LANES), lambda i, length_ref: (i, 0, 0)),
            ],
            scratch_shapes=[
                pltpu.VMEM((kv_local, block * stacked, HD), jnp.float32),
                pltpu.VMEM((kv_local, block * STEPS, HD), jnp.float32),
                pltpu.VMEM((kv_local, block * STEPS, HD), jnp.float32),
            ],
        ),
        out_shape=[
            jax.ShapeDtypeStruct(queries.shape, jnp.float32),
            jax.ShapeDtypeStruct((rows, STEPS, LANES), jnp.float32),
        ],
        compiler_params=pltpu.CompilerParams(vmem_limit_bytes=VMEM_BYTES),
        cost_estimate=pl.CostEstimate(
            flops=4 * rows * heads * STEPS * HD * context,
            bytes_accessed=4 * rows * context * width,
            transcendentals=rows * heads * STEPS * context,
        ),
        name="cached_attention",
    )(lengths, queries, cache_keys, cache_values, step_keys, step_values)


def visual_attention(places, queries, pairs):
    images = places.shape[1]
    slots, _, full = queries.shape
    heads = full // HD
    kv_local = pairs.shape[1] // (2 * HD)
    group = heads // kv_local
    stacked = group * STEPS
    window = VMAX + 16
    scale = HD**-0.5

    def kernel(place_ref, q_ref, pair_ref, out_ref, q_s, score_s, weight_s):
        for i in range(images):
            slot = place_ref[0, i]
            for h in range(heads):
                q_s[i, h * STEPS : (h + 1) * STEPS, :] = q_ref[
                    slot, :, h * HD : (h + 1) * HD
                ].astype(jnp.float32)
        for i in range(images):
            rows = pl.ds(pl.multiple_of(place_ref[1, i], 16), window)
            q = q_s[i].astype(jnp.bfloat16)
            for g in range(kv_local):
                score_s[i, g * stacked : (g + 1) * stacked, :] = dot_t(
                    q[g * stacked : (g + 1) * stacked], pair_ref[rows, g * HD : (g + 1) * HD]
                )
        column = lax.broadcasted_iota(jnp.int32, (heads * STEPS, window), 1)
        inverses = []
        logs = []
        for i in range(images):
            start = place_ref[2, i]
            live = (column >= start) & (column < start + place_ref[3, i])
            scores = jnp.where(live, score_s[i] * scale, FLOOR)
            peak = jnp.max(scores, axis=1, keepdims=True)
            weights = jnp.exp(scores - peak)
            total = jnp.sum(weights, axis=1, keepdims=True)
            weight_s[i] = weights.astype(jnp.bfloat16)
            inverses.append(1.0 / total)
            logs.append(jnp.broadcast_to(peak + jnp.log(total), (heads * STEPS, LANES)))
        lane = lax.broadcasted_iota(jnp.int32, (STEPS, LANES), 1)
        for i in range(images):
            slot = place_ref[0, i]
            rows = pl.ds(pl.multiple_of(place_ref[1, i], 16), window)
            high_part = jnp.zeros((STEPS, LANES), jnp.float32)
            for g in range(kv_local):
                at = (kv_local + g) * HD
                part = dot(
                    weight_s[i, g * stacked : (g + 1) * stacked, :], pair_ref[rows, at : at + HD]
                )
                part = part * inverses[i][g * stacked : (g + 1) * stacked]
                for j in range(group):
                    h = g * group + j
                    out_ref[slot, :, h * HD : (h + 1) * HD] = part[
                        j * STEPS : (j + 1) * STEPS
                    ].astype(out_ref.dtype)
            packed = jnp.zeros((STEPS, LANES), jnp.float32)
            for h in range(heads):
                log = logs[i][h * STEPS : (h + 1) * STEPS]
                packed = jnp.where(lane % heads == h, log, packed)
            first = packed.astype(jnp.bfloat16).astype(jnp.float32)
            rest = packed - first
            second = rest.astype(jnp.bfloat16).astype(jnp.float32)
            third = rest - second
            out_ref[slot, :, full:] = jnp.where(
                lane < heads,
                first,
                jnp.where(lane < 2 * heads, second, jnp.where(lane < 3 * heads, third, 0.0)),
            ).astype(out_ref.dtype)

    vmem = pl.BlockSpec(memory_space=pltpu.VMEM)
    return pl.pallas_call(
        kernel,
        in_specs=[pl.BlockSpec(memory_space=pltpu.SMEM), vmem, vmem],
        out_specs=vmem,
        out_shape=jax.ShapeDtypeStruct((slots, STEPS, full + LANES), queries.dtype),
        scratch_shapes=[
            pltpu.VMEM((images, heads * STEPS, HD), jnp.float32),
            pltpu.VMEM((images, heads * STEPS, window), jnp.float32),
            pltpu.VMEM((images, heads * STEPS, window), jnp.bfloat16),
        ],
        compiler_params=pltpu.CompilerParams(vmem_limit_bytes=VMEM_BYTES),
        name="visual_attention",
    )(places, queries, pairs)


def merge(slot_of_row, returned, cached, cached_log):
    rows, _, full = cached.shape
    heads = full // HD

    def kernel(slot_ref, returned_ref, cached_ref, log_ref, out_ref):
        for r in range(rows):
            slot = slot_ref[r]
            present = slot >= 0
            slot = jnp.maximum(slot, 0)
            terms = returned_ref[slot, :, full:].astype(jnp.float32)
            for h in range(heads):
                log = (
                    terms[:, h : h + 1]
                    + terms[:, heads + h : heads + h + 1]
                    + terms[:, 2 * heads + h : 2 * heads + h + 1]
                )
                share = 1.0 / (1.0 + jnp.exp(log_ref[r, :, h : h + 1] - log))
                own = cached_ref[r, :, h * HD : (h + 1) * HD]
                other = returned_ref[slot, :, h * HD : (h + 1) * HD].astype(jnp.float32)
                mixed = own + jnp.where(present, share * (other - own), 0.0)
                out_ref[r, :, h * HD : (h + 1) * HD] = mixed.astype(out_ref.dtype)

    vmem = pl.BlockSpec(memory_space=pltpu.VMEM)
    return pl.pallas_call(
        kernel,
        in_specs=[pl.BlockSpec(memory_space=pltpu.SMEM), vmem, vmem, vmem],
        out_specs=vmem,
        out_shape=jax.ShapeDtypeStruct(cached.shape, jnp.bfloat16),
        compiler_params=pltpu.CompilerParams(vmem_limit_bytes=VMEM_BYTES),
        name="merge",
    )(slot_of_row, returned, cached, cached_log)


def shards(
    visual_tokens,
    kv_weight,
    image_lengths,
    image_owner,
    cache_lengths,
    cache_keys,
    cache_values,
    step_queries,
    step_keys,
    step_values,
):
    devices = lax.axis_size("dp")
    rows_local = cache_lengths.shape[0]
    images_local = image_lengths.shape[1]
    capacity = -(-rows_local // devices)
    width_local = cache_keys.shape[2]
    weight_half = kv_weight[0]
    tensor = lax.axis_index("tensor").astype(jnp.int32)

    packed, slot_of_row = pack_queries(image_owner, step_queries, devices, capacity)
    asked = lax.all_to_all(packed, "dp", split_axis=0, concat_axis=0, tiled=True)

    for_partner = project(visual_tokens, weight_half, 1 - tensor, True)
    from_partner = lax.ppermute(for_partner, "tensor", [(0, 1), (1, 0)])
    own = project(visual_tokens, weight_half, tensor, False)

    cached, cached_log = cached_attention(
        step_queries, cache_keys, cache_values, step_keys, step_values, cache_lengths
    )

    device = lax.axis_index("dp")
    own_lengths = lax.dynamic_index_in_dim(image_lengths, device, 0, keepdims=False)
    own_device = (
        lax.dynamic_slice_in_dim(image_owner, device * images_local, images_local) // rows_local
    )
    order = jnp.arange(images_local)
    earlier = order[None, :] < order[:, None]
    own_rank = jnp.sum(
        ((own_device[:, None] == own_device[None, :]) & earlier).astype(jnp.int32), axis=1
    )
    starts = jnp.sum(jnp.where(earlier, own_lengths[None, :], 0), axis=1)
    window_at = jnp.minimum(starts // 16 * 16, visual_tokens.shape[0] - VMAX - 16)
    places = jnp.stack([own_device * capacity + own_rank, window_at, starts - window_at, own_lengths])

    split = 2 * width_local
    squares = for_partner[:, split : split + 1] + from_partner[:, split : split + 1]
    pairs = (own + from_partner[:, :split]) * lax.rsqrt(squares / D + EPSILON)
    pairs = pairs.astype(jnp.bfloat16)

    answers = visual_attention(places, asked, pairs)
    returned = lax.all_to_all(answers, "dp", split_axis=0, concat_axis=0, tiled=True)
    return merge(slot_of_row, returned, cached, cached_log)


def solution(mesh):
    return jax.shard_map(
        shards,
        mesh=mesh,
        in_specs=(
            P(("groups", "dp"), "tensor"),
            P("tensor", None, None, None),
            P("groups", None),
            P("groups"),
            P(("groups", "dp")),
            P(("groups", "dp"), None, "tensor"),
            P(("groups", "dp"), None, "tensor"),
            P(("groups", "dp"), None, "tensor"),
            P(("groups", "dp"), None, "tensor"),
            P(("groups", "dp"), None, "tensor"),
        ),
        out_specs=P(("groups", "dp"), None, "tensor"),
        check_vma=False,
    )
```

time: 327 us -> 66.1 us (0.20)
  waiting for transfers between devices: 210 us -> 9 us
  Pallas kernels: 0 us -> 30 us
  other arithmetic: 29.9 us -> 0.85 us
  local copies, waits for them, and re-layouts: 40.3 us -> 14.5 us
  matrix products: 22.2 us -> 0 us
  between operations: 13.7 us -> 0.19 us
  starting transfers between devices: 7.51 us -> 11 us
    all_to_all x1 -> x2, waiting for transfers between devices: 205 us -> 9 us  [the longest x1 6.21 us: shards(): lax.all_to_all(answers, 'dp', split_axis=0, concat_axis=0, tiled=True)]
    gather x2 -> x0, local copies, waits for them, and re-layouts: 30.6 us -> none  [the longest x1 21.1 us: shards(): taken = jnp.take(normed, send_index, axis=0)]
    pallas_call x0 -> x6, Pallas kernels: none -> 30 us  [the longest x1 14.5 us: pack_queries(): pl.pallas_call(kernel, in_specs=[pl.BlockSpec(memory_space=pltpu.SMEM), p...]
    dot_general x2 -> x0, matrix products: 17.9 us -> none  [the longest x1 15.8 us: shards(): jnp.einsum('td,dcf->tcf', arrived, weight_half, preferred_element_type=jn...]
    select_n x5 -> x1, other arithmetic: 17.5 us -> 0.09 us  [shards(): lax.dynamic_slice_in_dim(image_owner, device * images_local, images_local)]
    unnamed x18 -> x30, local copies, waits for them, and re-layouts: 3.21 us -> 14.5 us
    convert_element_type x2 -> x1, other arithmetic: 7.16 us -> 0.2 us  [shards(): pairs = pairs.astype(jnp.bfloat16)]
    reduce_scatter x1 -> x0, waiting for transfers between devices: 4.85 us -> none  [shards(): lax.psum_scatter(partial_value, 'tensor', scatter_dimension=2, tiled=True)]
  transfers between devices with their start and end apart: 2 -> 3, of which waited for: 2 -> 2; matrix products, arithmetic and copies ran while one was open for 2% -> 1% of each run, Pallas kernels for 0% -> 33%
where the time goes in v1:
time: 66.1 us; the launch traced here: 65.6 us
  Pallas kernels  30 us (45%)
  local copies, waits for them, and re-layouts  14.5 us (22%)
  starting transfers between devices  11 us (17%)
  waiting for transfers between devices  9 us (14%)
  other arithmetic  0.85 us (1%)
    unnamed x30, local copies, waits for them, and re-layouts  14.5 us
    pallas_call x1, Pallas kernels, pack_queries(): pl.pallas_call(kernel, in_specs=[pl.BlockSpec(memory_space=pltpu.SMEM), p...  14.5 us
    all_to_all x1, starting transfers between devices, shards(): lax.all_to_all(packed, 'dp', split_axis=0, concat_axis=0, tiled=True)  6.85 us
    pallas_call x2, Pallas kernels, project(): pl.pallas_call(kernel, grid_spec=pltpu.PrefetchScalarGridSpec(num_scalar_...  6.77 us
    all_to_all x1, waiting for transfers between devices, shards(): lax.all_to_all(answers, 'dp', split_axis=0, concat_axis=0, tiled=True)  6.21 us
    pallas_call x1, Pallas kernels, cached_attention(): pl.pallas_call(kernel, grid_spec=pltpu.PrefetchScalarGridSpec(num_scalar_...  3.82 us
    all_to_all x1, starting transfers between devices, shards(): lax.all_to_all(answers, 'dp', split_axis=0, concat_axis=0, tiled=True)  3.64 us
    pallas_call x1, Pallas kernels, merge(): pl.pallas_call(kernel, in_specs=[pl.BlockSpec(memory_space=pltpu.SMEM), v...  2.97 us
  transfers between devices with their start and end apart: 3, of which 2 were waited for; matrix products, arithmetic and copies ran while one was open for 1% of the time, Pallas kernels for 33%

profile of v1, /device:TPU:0, one launch (start us, length us, event | category | flops | bytes accessed | tf_op | source)
XLA Modules:
  0.0 65.6 jit_solution(7513010756984664471)
XLA Ops:
  0.0 0.0 copy-start
  0.0 0.0 copy-start.1
  0.0 3.4 %copy-done.1 = bf16[1,4096,2,512]{3,2,1,0:T(2,128)(2,1)S(1)} copy-done((bf16[1,4096,2,512]{3,2,1,0:T(2,128)(2,1)S(1)}, bf16[1,4096,2,512]{3,2,1,0:T(2,128)(2,1)}, u32[]{:S(2)}) %copy-start.1) | copy-done | bytes 8388632
  3.4 0.0 copy-start.3
  3.4 2.1 %copy-done.3 = bf16[480,4096]{1,0:T(8,128)(2,1)S(1)} copy-done((bf16[480,4096]{1,0:T(8,128)(2,1)S(1)}, bf16[480,4096]{1,0:T(8,128)(2,1)}, u32[]{:S(2)}) %copy-start.3) | copy-done | bytes 3932184
  5.5 0.0 copy-start.14
  5.5 3.7 %project_partner.1 = f32[480,640]{1,0:T(8,128)S(1)} custom-call(s32[1]{0:T(128)} %bitcast.5.half_ref, bf16[480,4096]{1,0:T(8,128)(2,1)S(1)} %copy-done.3, bf16[4096,2,512]{2,1,0:T(2,128)(2,1)S(1)} %bitcast.20), custom_call_target="tpu_custom_call" | custom-call | flops 2013265920 | bytes 8126464 | tf_op jit(solution)/shard_map/project_partner/pallas_call | solution.py:102
  9.2 0.5 collective-permute-start
  9.8 14.5 %pack_queries.1 = (bf16[24,4,2048]{2,1,0:T(4,128)(2,1)}, s32[25]{0:T(128)}) custom-call(s32[96]{0:T(128)} %owner.1, bf16[24,4,2048]{2,1,0:T(4,128)(2,1)} %q_ref.1), custom_call_target="tpu_custom_call" | custom-call | tf_op jit(solution)/shard_map/pack_queries/pallas_call | solution.py:57
  24.2 6.8 %all-to-all-start = ((bf16[24,4,2048]{2,1,0:T(4,128)(2,1)}), bf16[24,4,2048]{2,1,0:T(4,128)(2,1)S(1)}, u32[]{:S(2)}, u32[]{:S(2)}) async-start(bf16[24,4,2048]{2,1,0:T(4,128)(2,1)} %get-tuple-element.10), calls=%async_computation | async-start | bytes 786432 | tf_op jit(solution)/shard_map/all_to_all | solution.py:367
  31.1 0.0 copy-done
  31.1 0.0 copy-done.14
  31.1 0.1 and_select_fusion.1
  31.2 0.1 select_reduce_fusion
  31.3 0.2 convert_reduce_fusion
  31.5 0.1 add_bitcast_fusion
  31.6 0.0 copy-start.2
  31.7 3.4 %copy-done.2 = bf16[1,4096,2,512]{3,2,1,0:T(2,128)(2,1)S(1)} copy-done((bf16[1,4096,2,512]{3,2,1,0:T(2,128)(2,1)S(1)}, bf16[1,4096,2,512]{3,2,1,0:T(2,128)(2,1)}, u32[]{:S(2)}) %copy-start.2) | copy-done | bytes 8388632
  35.0 0.0 copy-start.4
  35.0 2.1 %copy-done.4 = bf16[480,4096]{1,0:T(8,128)(2,1)S(1)} copy-done((bf16[480,4096]{1,0:T(8,128)(2,1)S(1)}, bf16[480,4096]{1,0:T(8,128)(2,1)}, u32[]{:S(2)}) %copy-start.4) | copy-done | bytes 3932184
  37.1 3.1 %project_own.1 = f32[480,512]{1,0:T(8,128)S(1)} custom-call(s32[1]{0:T(128)} %bitcast.3.half_ref, bf16[480,4096]{1,0:T(8,128)(2,1)S(1)} %copy-done.4, bf16[4096,2,512]{2,1,0:T(2,128)(2,1)S(1)} %bitcast.21), custom_call_target="tpu_custom_call" | custom-call | flops 2013265920 | bytes 8126464 | tf_op jit(solution)/shard_map/project_own/pallas_call | solution.py:102
  40.2 0.0 collective-permute-done
  40.2 0.2 fusion.5
  40.4 0.2 fusion.1.pair_ref
  40.6 0.0 copy-start.5
  40.6 0.0 copy-start.7
  40.6 0.0 copy-start.10
  40.6 0.0 copy-start.11
  40.6 0.0 copy-start.13
  40.6 2.8 %all-to-all-done.q_ref = bf16[24,4,2048]{2,1,0:T(4,128)(2,1)S(1)} async-done(((bf16[24,4,2048]{2,1,0:T(4,128)(2,1)}), bf16[24,4,2048]{2,1,0:T(4,128)(2,1)S(1)}, u32[]{:S(2)}, u32[]{:S(2)}) %all-to-all-start) | async-done | bytes 393248 | tf_op jit(solution)/shard_map/all_to_all | solution.py:367
  43.4 2.0 %visual_attention.1 = bf16[24,4,2176]{2,1,0:T(4,128)(2,1)} custom-call(s32[4,12]{1,0:T(4,128)S(1)} %pad_add_fusion.place_ref, bf16[24,4,2048]{2,1,0:T(4,128)(2,1)S(1)} %all-to-all-done.q_ref, bf16[480,512]{1,0:T(8,128)(2,1)S(1)} %fusion.1.pair_ref), custom_call_target="tpu_custom_call" | custom-call | tf_op jit(solution)/shard_map/visual_attention/pallas_call | solution.py:298
  45.4 3.6 %all-to-all-start.1 = ((bf16[24,4,2176]{2,1,0:T(4,128)(2,1)}), bf16[24,4,2176]{2,1,0:T(4,128)(2,1)S(1)}, u32[]{:S(2)}, u32[]{:S(2)}) async-start(bf16[24,4,2176]{2,1,0:T(4,128)(2,1)} %visual_attention.1), calls=%async_computation.1 | async-start | bytes 835584 | tf_op jit(solution)/shard_map/all_to_all | solution.py:397
  49.1 0.0 copy-done.5
  49.1 0.0 copy-done.7
  49.1 0.0 copy-done.10
  49.1 0.0 copy-done.11
  49.1 0.0 copy-done.13
  49.1 0.0 copy-start.6
  49.1 1.4 %copy-done.6 = bf16[24,128,256]{2,1,0:T(8,128)(2,1)S(1)} copy-done((bf16[24,128,256]{2,1,0:T(8,128)(2,1)S(1)}, bf16[24,128,256]{2,1,0:T(8,128)(2,1)}, u32[]{:S(2)}) %copy-start.6) | copy-done | bytes 1572888
  50.5 0.0 copy-start.12
  50.5 3.8 %cached_attention.1 = (f32[24,4,2048]{2,1,0:T(4,128)S(1)}, f32[24,4,128]{2,1,0:T(4,128)S(1)}) custom-call(s32[24]{0:T(128)S(1)} %copy-done.13, bf16[24,4,2048]{2,1,0:T(4,128)(2,1)S(1)} %copy-done.7, bf16[24,128,256]{2,1,0:T(8,128)(2,1)S(1)} %copy-done.5, bf16[24,128,256]{2,1,0:T(8,128)(2,1)S(1)} %copy-done.6, bf16[24,4,256]{2,1,0:T(4,128)(2,1)S(1)} %copy-done.10, ...), custom_call_target="tpu_custom_call" | custom-call | flops 100663296 | bytes 3145728 | tf_op jit(solution)/shard_map/cached_attention/pallas_call | solution.py:194
  54.3 0.0 copy-start.8
  54.4 0.9 %copy-done.8 = f32[24,4,2048]{2,1,0:T(4,128)} copy-done((f32[24,4,2048]{2,1,0:T(4,128)}, f32[24,4,2048]{2,1,0:T(4,128)S(1)}, u32[]{:S(2)}) %copy-start.8) | copy-done | bytes 786456
  55.3 6.2 %all-to-all-done.1.returned_ref = bf16[24,4,2176]{2,1,0:T(4,128)(2,1)S(1)} async-done(((bf16[24,4,2176]{2,1,0:T(4,128)(2,1)}), bf16[24,4,2176]{2,1,0:T(4,128)(2,1)S(1)}, u32[]{:S(2)}, u32[]{:S(2)}) %all-to-all-start.1) | async-done | bytes 417824 | tf_op jit(solution)/shard_map/all_to_all | solution.py:397
  61.5 0.0 copy-done.12
  61.5 0.0 copy-start.9
  61.5 1.1 %copy-done.9 = f32[24,4,2048]{2,1,0:T(4,128)S(1)} copy-done((f32[24,4,2048]{2,1,0:T(4,128)S(1)}, f32[24,4,2048]{2,1,0:T(4,128)}, u32[]{:S(2)}) %copy-start.9) | copy-done | bytes 786456
  62.6 3.0 %merge.1 = bf16[24,4,2048]{2,1,0:T(4,128)(2,1)} custom-call(s32[25]{0:T(128)S(1)} %copy-done.12, bf16[24,4,2176]{2,1,0:T(4,128)(2,1)S(1)} %all-to-all-done.1.returned_ref, f32[24,4,2048]{2,1,0:T(4,128)S(1)} %copy-done.9, f32[24,4,128]{2,1,0:T(4,128)S(1)} %get-tuple-element.12.log_ref), custom_call_target="tpu_custom_call" | custom-call | tf_op jit(solution)/shard_map/merge/pallas_call | solution.py:336
  (4 shorter events, 0.0 us)
Async XLA Ops:
  0.0 31.1 %copy-start = (s32[8,12]{1,0:T(8,128)S(1)}, s32[8,12]{1,0:T(8,128)}, u32[]{:S(2)}) copy-start(s32[8,12]{1,0:T(8,128)} %param.12) | copy-start | bytes 1156
  0.0 3.4 %copy-start.1 = (bf16[1,4096,2,512]{3,2,1,0:T(2,128)(2,1)S(1)}, bf16[1,4096,2,512]{3,2,1,0:T(2,128)(2,1)}, u32[]{:S(2)}) copy-start(bf16[1,4096,2,512]{3,2,1,0:T(2,128)(2,1)} %param.11) | copy-start | bytes 25165828
  3.4 2.1 %copy-start.3 = (bf16[480,4096]{1,0:T(8,128)(2,1)S(1)}, bf16[480,4096]{1,0:T(8,128)(2,1)}, u32[]{:S(2)}) copy-start(bf16[480,4096]{1,0:T(8,128)(2,1)} %token_ref.3) | copy-start | bytes 11796484
  5.5 25.6 %copy-start.14 = (s32[96]{0:T(128)S(1)}, s32[96]{0:T(128)}, u32[]{:S(2)}) copy-start(s32[96]{0:T(128)} %owner.1) | copy-start | bytes 1156
  9.2 31.0 %collective-permute-start = (f32[480,640]{1,0:T(8,128)S(1)}, f32[480,640]{1,0:T(8,128)S(1)}, u32[]{:S(2)}, u32[]{:S(2)}) collective-permute-start(f32[480,640]{1,0:T(8,128)S(1)} %project_partner.1), channel_id=1, source_target_pairs={{0,1},{1,0},{2,3},{3,2},{4,5},{5,4},{6,7},{7,6},{8,9},{9,8},{10,11... | collective-permute-start | bytes 3686408 | tf_op jit(solution)/shard_map/ppermute | solution.py:370
  24.2 19.2 %all-to-all-start = ((bf16[24,4,2048]{2,1,0:T(4,128)(2,1)}), bf16[24,4,2048]{2,1,0:T(4,128)(2,1)S(1)}, u32[]{:S(2)}, u32[]{:S(2)}) async-start(bf16[24,4,2048]{2,1,0:T(4,128)(2,1)} %get-tuple-element.10), calls=%async_computation | async-start | bytes 786432 | tf_op jit(solution)/shard_map/all_to_all | solution.py:367
  31.6 3.4 %copy-start.2 = (bf16[1,4096,2,512]{3,2,1,0:T(2,128)(2,1)S(1)}, bf16[1,4096,2,512]{3,2,1,0:T(2,128)(2,1)}, u32[]{:S(2)}) copy-start(bf16[1,4096,2,512]{3,2,1,0:T(2,128)(2,1)} %param.11) | copy-start | bytes 25165828
  35.0 2.1 %copy-start.4 = (bf16[480,4096]{1,0:T(8,128)(2,1)S(1)}, bf16[480,4096]{1,0:T(8,128)(2,1)}, u32[]{:S(2)}) copy-start(bf16[480,4096]{1,0:T(8,128)(2,1)} %token_ref.3) | copy-start | bytes 11796484
  40.6 8.5 %copy-start.5 = (bf16[24,128,256]{2,1,0:T(8,128)(2,1)S(1)}, bf16[24,128,256]{2,1,0:T(8,128)(2,1)}, u32[]{:S(2)}) copy-start(bf16[24,128,256]{2,1,0:T(8,128)(2,1)} %k_ref.1) | copy-start | bytes 4718596
  40.6 8.5 %copy-start.7 = (bf16[24,4,2048]{2,1,0:T(4,128)(2,1)S(1)}, bf16[24,4,2048]{2,1,0:T(4,128)(2,1)}, u32[]{:S(2)}) copy-start(bf16[24,4,2048]{2,1,0:T(4,128)(2,1)} %q_ref.1) | copy-start | bytes 1179652
  40.6 8.5 %copy-start.10 = (bf16[24,4,256]{2,1,0:T(4,128)(2,1)S(1)}, bf16[24,4,256]{2,1,0:T(4,128)(2,1)}, u32[]{:S(2)}) copy-start(bf16[24,4,256]{2,1,0:T(4,128)(2,1)} %sk_ref.1) | copy-start | bytes 147460
  40.6 8.5 %copy-start.11 = (bf16[24,4,256]{2,1,0:T(4,128)(2,1)S(1)}, bf16[24,4,256]{2,1,0:T(4,128)(2,1)}, u32[]{:S(2)}) copy-start(bf16[24,4,256]{2,1,0:T(4,128)(2,1)} %sv_ref.1) | copy-start | bytes 147460
  40.6 8.5 %copy-start.13 = (s32[24]{0:T(128)S(1)}, s32[24]{0:T(128)}, u32[]{:S(2)}) copy-start(s32[24]{0:T(128)} %length_ref.1) | copy-start | bytes 292
  45.4 16.1 %all-to-all-start.1 = ((bf16[24,4,2176]{2,1,0:T(4,128)(2,1)}), bf16[24,4,2176]{2,1,0:T(4,128)(2,1)S(1)}, u32[]{:S(2)}, u32[]{:S(2)}) async-start(bf16[24,4,2176]{2,1,0:T(4,128)(2,1)} %visual_attention.1), calls=%async_computation.1 | async-start | bytes 835584 | tf_op jit(solution)/shard_map/all_to_all | solution.py:397
  49.1 1.4 %copy-start.6 = (bf16[24,128,256]{2,1,0:T(8,128)(2,1)S(1)}, bf16[24,128,256]{2,1,0:T(8,128)(2,1)}, u32[]{:S(2)}) copy-start(bf16[24,128,256]{2,1,0:T(8,128)(2,1)} %v_ref.1) | copy-start | bytes 4718596
  50.5 11.0 %copy-start.12 = (s32[25]{0:T(128)S(1)}, s32[25]{0:T(128)}, u32[]{:S(2)}) copy-start(s32[25]{0:T(128)} %get-tuple-element.9.slot_ref) | copy-start | bytes 304
  54.3 0.9 %copy-start.8 = (f32[24,4,2048]{2,1,0:T(4,128)}, f32[24,4,2048]{2,1,0:T(4,128)S(1)}, u32[]{:S(2)}) copy-start(f32[24,4,2048]{2,1,0:T(4,128)S(1)} %get-tuple-element.11.cached_ref) | copy-start | bytes 2359300
  61.5 1.1 %copy-start.9 = (f32[24,4,2048]{2,1,0:T(4,128)S(1)}, f32[24,4,2048]{2,1,0:T(4,128)}, u32[]{:S(2)}) copy-start(f32[24,4,2048]{2,1,0:T(4,128)} %copy-done.8) | copy-start | bytes 2359300

commit v2 on v1

v2 whole, which is shorter than its diff:
```python
import jax
import jax.numpy as jnp
from jax import lax
from jax.experimental import pallas as pl
from jax.experimental.pallas import tpu as pltpu
from jax.sharding import PartitionSpec as P

D = 8192
HD = 128
STEPS = 4
VMAX = 48
EPSILON = 1e-06
LANES = 128
FLOOR = -1e30
PIECES = 4
FAR_BYTES = 40 << 20


def dot_t(a, b):
    return lax.dot_general(a, b, (((1,), (1,)), ((), ())), preferred_element_type=jnp.float32)


def dot(a, b):
    return jnp.dot(a, b, preferred_element_type=jnp.float32)


def pack_queries(image_owner, step_queries, devices, capacity):
    rows = step_queries.shape[0]
    images = image_owner.shape[0] // devices
    slots = devices * capacity

    def kernel(owner_hbm, query_hbm, packed, slot_of_row, owner, queries, row_of_slot, in_sems, sems):
        read_owner = pltpu.make_async_copy(owner_hbm, owner, in_sems.at[0])
        read_queries = pltpu.make_async_copy(query_hbm, queries, in_sems.at[1])
        read_owner.start()
        read_queries.start()
        base = lax.axis_index("dp") * rows
        for r in range(rows):
            slot_of_row[r] = -1
        for slot in range(slots):
            row_of_slot[slot] = 0
        read_owner.wait()
        copies = []
        for s in range(devices):
            rank = jnp.int32(0)
            for i in range(images):
                row = owner[s * images + i] - base
                local = jnp.logical_and(row >= 0, row < rows)
                slot = s * capacity + rank
                row_of_slot[jnp.where(local, slot, slots)] = row
                slot_of_row[jnp.where(local, row, rows)] = slot
                rank = rank + local.astype(jnp.int32)
            if s == 0:
                read_queries.wait()
            for k in range(capacity):
                slot = s * capacity + k
                copy = pltpu.make_async_copy(
                    queries.at[row_of_slot[slot]], packed.at[slot], sems.at[slot]
                )
                copy.start()
                copies.append(copy)
        for copy in copies:
            copy.wait()

    return pl.pallas_call(
        kernel,
        in_specs=[pl.BlockSpec(memory_space=pl.ANY), pl.BlockSpec(memory_space=pl.ANY)],
        out_specs=[pl.BlockSpec(memory_space=pl.ANY), pl.BlockSpec(memory_space=pltpu.SMEM)],
        out_shape=[
            jax.ShapeDtypeStruct((slots,) + step_queries.shape[1:], step_queries.dtype),
            jax.ShapeDtypeStruct((rows + 1,), jnp.int32),
        ],
        scratch_shapes=[
            pltpu.SMEM(image_owner.shape, jnp.int32),
            pltpu.VMEM(step_queries.shape, step_queries.dtype),
            pltpu.SMEM((slots + 1,), jnp.int32),
            pltpu.SemaphoreType.DMA((2,)),
            pltpu.SemaphoreType.DMA((slots,)),
        ],
        name="pack_queries",
    )(image_owner, step_queries)


def project(tokens, weight):
    count, depth = tokens.shape
    width = weight.shape[2] // 2
    columns = 2 * width + LANES
    piece = count // PIECES
    sizes = [512, 512] + [1024] * ((depth - 1024) // 1024)
    starts = [sum(sizes[:c]) for c in range(len(sizes))]
    chunks = len(sizes)
    ahead = 3

    def kernel(token_hbm, weight_hbm, *refs):
        pieces = refs[:PIECES]
        ours_hbm, theirs_s, ours_s, token_s, weight_s, sems, out_sems = refs[PIECES:]
        mine = lax.axis_index("tensor")

        def lanes(half):
            return pl.ds(pl.multiple_of(half * width, width), width)

        def product(x, w):
            w = jnp.swapaxes(w, 0, 1)
            return dot(x, jnp.concatenate([w[0], w[1]], axis=1))

        loads = []
        for c in range(chunks):
            span = pl.ds(starts[c], sizes[c])
            loads.append(
                [
                    pltpu.make_async_copy(
                        token_hbm.at[:, span], token_s.at[:, span], sems.at[0, c]
                    ),
                    pltpu.make_async_copy(
                        weight_hbm.at[span, :, lanes(1 - mine)],
                        weight_s.at[0, span],
                        sems.at[1, c],
                    ),
                ]
            )
        loads.append(
            [pltpu.make_async_copy(weight_hbm.at[:, :, lanes(mine)], weight_s.at[1], sems.at[2, 0])]
        )

        def start(c):
            if c < len(loads):
                for load in loads[c]:
                    load.start()

        for c in range(ahead):
            start(c)
        squares = jnp.zeros((count, LANES), jnp.float32)
        for c in range(chunks):
            for load in loads[c]:
                load.wait()
            start(c + ahead)
            span = slice(starts[c], starts[c] + sizes[c])
            x = token_s[:, span]
            part = product(x, weight_s[0, span])
            if c == 0:
                theirs_s[:, : 2 * width] = part
            else:
                theirs_s[:, : 2 * width] += part
            for lane in range(0, sizes[c], LANES):
                wide = x[:, lane : lane + LANES].astype(jnp.float32)
                squares += wide * wide
        squares = jnp.broadcast_to(jnp.sum(squares, axis=1, keepdims=True), (count, LANES))
        theirs_s[:, 2 * width :] = squares
        stores = []
        for k in range(PIECES):
            store = pltpu.make_async_copy(
                theirs_s.at[pl.ds(k * piece, piece)], pieces[k], out_sems.at[k]
            )
            store.start()
            stores.append(store)
        ours_s[:, 2 * width :] = squares
        for load in loads[chunks]:
            load.wait()
        ours_s[:, : 2 * width] = product(token_s[...], weight_s[1])
        store = pltpu.make_async_copy(
            ours_s, ours_hbm.at[pl.ds(0, count)], out_sems.at[PIECES]
        )
        store.start()
        stores.append(store)
        for store in stores:
            store.wait()

    hbm = pl.BlockSpec(memory_space=pltpu.HBM)
    *theirs, ours = pl.pallas_call(
        kernel,
        in_specs=[hbm, hbm],
        out_specs=[pl.BlockSpec(memory_space=pl.ANY)] * (PIECES + 1),
        out_shape=[jax.ShapeDtypeStruct((piece, columns), jnp.float32)] * PIECES
        + [jax.ShapeDtypeStruct((FAR_BYTES // (4 * columns), columns), jnp.float32)],
        scratch_shapes=[
            pltpu.VMEM((count, columns), jnp.float32),
            pltpu.VMEM((count, columns), jnp.float32),
            pltpu.VMEM(tokens.shape, tokens.dtype),
            pltpu.VMEM((2, depth, 2, width), weight.dtype),
            pltpu.SemaphoreType.DMA((3, chunks)),
            pltpu.SemaphoreType.DMA((PIECES + 1,)),
        ],
        compiler_params=pltpu.CompilerParams(vmem_limit_bytes=60 << 20),
        cost_estimate=pl.CostEstimate(flops=1 << 20, bytes_accessed=1 << 16, transcendentals=0),
        name="project",
    )(tokens, weight)
    return theirs, ours


def cached_attention(queries, cache_keys, cache_values, step_keys, step_values, lengths):
    rows, context, width = cache_keys.shape
    kv_local = width // HD
    heads = queries.shape[2] // HD
    group = heads // kv_local
    stacked = group * STEPS
    block = 8 if rows % 8 == 0 else 2
    scale = HD**-0.5

    def kernel(length_ref, q_ref, k_ref, v_ref, sk_ref, sv_ref, out_ref, q_s, sk_s, sv_s):
        first = pl.program_id(0) * block
        for r in range(block):
            for g in range(kv_local):
                sk_s[g, r * STEPS : (r + 1) * STEPS, :] = sk_ref[
                    r, :, g * HD : (g + 1) * HD
                ].astype(jnp.float32)
                sv_s[g, r * STEPS : (r + 1) * STEPS, :] = sv_ref[
                    r, :, g * HD : (g + 1) * HD
                ].astype(jnp.float32)
                for j in range(group):
                    h = g * group + j
                    at = r * stacked + j * STEPS
                    q_s[g, at : at + STEPS, :] = q_ref[r, :, h * HD : (h + 1) * HD].astype(
                        jnp.float32
                    )
        lane = lax.broadcasted_iota(jnp.int32, (STEPS, LANES), 1)
        logs = [jnp.zeros((STEPS, LANES), jnp.float32) for _ in range(block)]
        for g in range(kv_local):
            q = q_s[g].astype(jnp.bfloat16)
            steps = dot_t(q, sk_s[g].astype(jnp.bfloat16)) * scale
            at_row = lax.broadcasted_iota(jnp.int32, steps.shape, 0)
            at_key = lax.broadcasted_iota(jnp.int32, steps.shape, 1)
            own = (at_row // stacked == at_key // STEPS) & (at_key % STEPS <= at_row % STEPS)
            steps = jnp.where(own, steps, FLOOR)
            step_peak = jnp.max(steps, axis=1, keepdims=True)
            scores = []
            position = lax.broadcasted_iota(jnp.int32, (stacked, context), 1)
            for r in range(block):
                part = dot_t(q[r * stacked : (r + 1) * stacked], k_ref[r, :, g * HD : (g + 1) * HD])
                scores.append(jnp.where(position < length_ref[first + r], part * scale, FLOOR))
            cached = jnp.concatenate(scores, axis=0)
            peak = jnp.maximum(jnp.max(cached, axis=1, keepdims=True), step_peak)
            cached = jnp.exp(cached - peak)
            steps = jnp.where(own, jnp.exp(steps - peak), 0.0)
            total = jnp.sum(cached, axis=1, keepdims=True) + jnp.sum(steps, axis=1, keepdims=True)
            cached = cached.astype(jnp.bfloat16)
            mixed = dot(steps.astype(jnp.bfloat16), sv_s[g].astype(jnp.bfloat16))
            inverse = 1.0 / total
            log = jnp.broadcast_to(peak + jnp.log(total), (block * stacked, LANES))
            for r in range(block):
                span = slice(r * stacked, (r + 1) * stacked)
                part = dot(cached[span], v_ref[r, :, g * HD : (g + 1) * HD])
                part = (part + mixed[span]) * inverse[span]
                for j in range(group):
                    h = g * group + j
                    head = slice(j * STEPS, (j + 1) * STEPS)
                    out_ref[r, :, h * HD : (h + 1) * HD] = part[head]
                    at = r * stacked + j * STEPS
                    logs[r] = jnp.where(lane == h, log[at : at + STEPS], logs[r])
        for r in range(block):
            out_ref[r, :, heads * HD :] = logs[r]

    def spec(array):
        return pl.BlockSpec((block,) + array.shape[1:], lambda i, length_ref: (i, 0, 0))

    return pl.pallas_call(
        kernel,
        grid_spec=pltpu.PrefetchScalarGridSpec(
            num_scalar_prefetch=1,
            grid=(rows // block,),
            in_specs=[
                spec(queries),
                spec(cache_keys),
                spec(cache_values),
                spec(step_keys),
                spec(step_values),
            ],
            out_specs=pl.BlockSpec(
                (block, STEPS, heads * HD + LANES), lambda i, length_ref: (i, 0, 0)
            ),
            scratch_shapes=[
                pltpu.VMEM((kv_local, block * stacked, HD), jnp.float32),
                pltpu.VMEM((kv_local, block * STEPS, HD), jnp.float32),
                pltpu.VMEM((kv_local, block * STEPS, HD), jnp.float32),
            ],
        ),
        out_shape=jax.ShapeDtypeStruct(
            (FAR_BYTES // (4 * STEPS * (heads * HD + LANES)), STEPS, heads * HD + LANES), jnp.float32
        ),
        compiler_params=pltpu.CompilerParams(vmem_limit_bytes=60 << 20),
        cost_estimate=pl.CostEstimate(flops=1 << 20, bytes_accessed=1 << 16, transcendentals=0),
        name="cached_attention",
    )(lengths, queries, cache_keys, cache_values, step_keys, step_values)


def visual_attention(places, queries, ours, received):
    images = places.shape[1]
    slots, _, full = queries.shape
    heads = full // HD
    columns = ours.shape[1]
    split = columns - LANES
    kv_local = split // (2 * HD)
    piece = received[0].shape[0]
    count = piece * PIECES
    group = heads // kv_local
    stacked = group * STEPS
    window = VMAX + 16
    scale = HD**-0.5

    def kernel(place_ref, q_ref, ours_hbm, *refs):
        received_hbm = refs[:PIECES]
        out_hbm, ours_s, received_s, pair_ref, q_s, score_s, weight_s, out_ref, load_sems, sems = refs[
            PIECES:
        ]
        loads = []
        for k in range(PIECES):
            rows = pl.ds(k * piece, piece)
            pair = (
                pltpu.make_async_copy(ours_hbm.at[rows], ours_s.at[rows], load_sems.at[0, k]),
                pltpu.make_async_copy(received_hbm[k], received_s.at[rows], load_sems.at[1, k]),
            )
            for load in pair:
                load.start()
            loads.append(pair)
        stores = []
        for i in range(images):
            slot = place_ref[0, i]
            for h in range(heads):
                q_s[i, h * STEPS : (h + 1) * STEPS, :] = q_ref[
                    slot, :, h * HD : (h + 1) * HD
                ].astype(jnp.float32)
        for k in range(PIECES):
            for load in loads[k]:
                load.wait()
            rows = slice(k * piece, (k + 1) * piece)
            factor = lax.rsqrt((ours_s[rows, split:] + received_s[rows, split:]) / D + EPSILON)
            for at in range(0, split, LANES):
                lanes = slice(at, at + LANES)
                total = (ours_s[rows, lanes] + received_s[rows, lanes]) * factor
                pair_ref[rows, lanes] = total.astype(pair_ref.dtype)
        for i in range(images):
            rows = pl.ds(pl.multiple_of(place_ref[1, i], 16), window)
            q = q_s[i].astype(jnp.bfloat16)
            for g in range(kv_local):
                score_s[i, g * stacked : (g + 1) * stacked, :] = dot_t(
                    q[g * stacked : (g + 1) * stacked], pair_ref[rows, g * HD : (g + 1) * HD]
                )
        column = lax.broadcasted_iota(jnp.int32, (heads * STEPS, window), 1)
        inverses = []
        logs = []
        for i in range(images):
            start = place_ref[2, i]
            live = (column >= start) & (column < start + place_ref[3, i])
            scores = jnp.where(live, score_s[i] * scale, FLOOR)
            peak = jnp.max(scores, axis=1, keepdims=True)
            weights = jnp.exp(scores - peak)
            total = jnp.sum(weights, axis=1, keepdims=True)
            weight_s[i] = weights.astype(jnp.bfloat16)
            inverses.append(1.0 / total)
            logs.append(jnp.broadcast_to(peak + jnp.log(total), (heads * STEPS, LANES)))
        lane = lax.broadcasted_iota(jnp.int32, (STEPS, LANES), 1)
        for i in range(images):
            rows = pl.ds(pl.multiple_of(place_ref[1, i], 16), window)
            for g in range(kv_local):
                at = (kv_local + g) * HD
                part = dot(
                    weight_s[i, g * stacked : (g + 1) * stacked, :], pair_ref[rows, at : at + HD]
                )
                part = part * inverses[i][g * stacked : (g + 1) * stacked]
                for j in range(group):
                    h = g * group + j
                    out_ref[i, :, h * HD : (h + 1) * HD] = part[
                        j * STEPS : (j + 1) * STEPS
                    ].astype(out_ref.dtype)
            packed = jnp.zeros((STEPS, LANES), jnp.float32)
            for h in range(heads):
                log = logs[i][h * STEPS : (h + 1) * STEPS]
                packed = jnp.where(lane % heads == h, log, packed)
            first = packed.astype(jnp.bfloat16).astype(jnp.float32)
            rest = packed - first
            second = rest.astype(jnp.bfloat16).astype(jnp.float32)
            third = rest - second
            out_ref[i, :, full:] = jnp.where(
                lane < heads,
                first,
                jnp.where(lane < 2 * heads, second, jnp.where(lane < 3 * heads, third, 0.0)),
            ).astype(out_ref.dtype)
            store = pltpu.make_async_copy(out_ref.at[i], out_hbm.at[place_ref[0, i]], sems.at[i])
            store.start()
            stores.append(store)
        for store in stores:
            store.wait()

    anywhere = pl.BlockSpec(memory_space=pl.ANY)
    return pl.pallas_call(
        kernel,
        in_specs=[
            pl.BlockSpec(memory_space=pltpu.SMEM),
            pl.BlockSpec(memory_space=pltpu.VMEM),
        ]
        + [anywhere] * (1 + PIECES),
        out_specs=anywhere,
        out_shape=jax.ShapeDtypeStruct((slots, STEPS, full + LANES), queries.dtype),
        scratch_shapes=[
            pltpu.VMEM((count, columns), jnp.float32),
            pltpu.VMEM((count, columns), jnp.float32),
            pltpu.VMEM((count, split), jnp.bfloat16),
            pltpu.VMEM((images, heads * STEPS, HD), jnp.float32),
            pltpu.VMEM((images, heads * STEPS, window), jnp.float32),
            pltpu.VMEM((images, heads * STEPS, window), jnp.bfloat16),
            pltpu.VMEM((images, STEPS, full + LANES), queries.dtype),
            pltpu.SemaphoreType.DMA((2, PIECES)),
            pltpu.SemaphoreType.DMA((images,)),
        ],
        compiler_params=pltpu.CompilerParams(vmem_limit_bytes=32 << 20),
        name="visual_attention",
    )(places, queries, ours, *received)


def merge(slot_of_row, returned, cached, rows):
    full = cached.shape[2] - LANES
    heads = full // HD
    runs = 3 if rows % 3 == 0 else 1
    run = rows // runs

    def kernel(slot_ref, returned_ref, cached_hbm, out_hbm, cached_s, out_s, sems):
        loads = []
        stores = []
        for k in range(runs):
            span = pl.ds(k * run, run)
            load = pltpu.make_async_copy(cached_hbm.at[span], cached_s.at[span], sems.at[0, k])
            load.start()
            loads.append(load)
        for k in range(runs):
            loads[k].wait()
            for r in range(k * run, (k + 1) * run):
                present = slot_ref[r] >= 0
                slot = jnp.maximum(slot_ref[r], 0)
                terms = returned_ref[slot, :, full:].astype(jnp.float32)
                log = (
                    terms[:, :heads] + terms[:, heads : 2 * heads] + terms[:, 2 * heads : 3 * heads]
                )
                share = 1.0 / (1.0 + jnp.exp(cached_s[r, :, full : full + heads] - log))
                for h in range(heads):
                    lanes = slice(h * HD, (h + 1) * HD)
                    own = cached_s[r, :, lanes]
                    other = returned_ref[slot, :, lanes].astype(jnp.float32)
                    mixed = own + share[:, h : h + 1] * (other - own)
                    out_s[r, :, lanes] = jnp.where(present, mixed, own).astype(out_s.dtype)
            span = pl.ds(k * run, run)
            store = pltpu.make_async_copy(out_s.at[span], out_hbm.at[span], sems.at[1, k])
            store.start()
            stores.append(store)
        for store in stores:
            store.wait()

    anywhere = pl.BlockSpec(memory_space=pl.ANY)
    return pl.pallas_call(
        kernel,
        in_specs=[
            pl.BlockSpec(memory_space=pltpu.SMEM),
            pl.BlockSpec(memory_space=pltpu.VMEM),
            anywhere,
        ],
        out_specs=anywhere,
        out_shape=jax.ShapeDtypeStruct((rows, STEPS, full), jnp.bfloat16),
        scratch_shapes=[
            pltpu.VMEM((rows, STEPS, full + LANES), jnp.float32),
            pltpu.VMEM((rows, STEPS, full), jnp.bfloat16),
            pltpu.SemaphoreType.DMA((2, runs)),
        ],
        compiler_params=pltpu.CompilerParams(vmem_limit_bytes=32 << 20),
        name="merge",
    )(slot_of_row, returned, cached)


def shards(
    visual_tokens,
    kv_weight,
    image_lengths,
    image_owner,
    cache_lengths,
    cache_keys,
    cache_values,
    step_queries,
    step_keys,
    step_values,
):
    devices = lax.axis_size("dp")
    rows_local = cache_lengths.shape[0]
    images_local = image_lengths.shape[1]
    capacity = -(-rows_local // devices)
    weight_half = kv_weight[0]
    packed, slot_of_row = pack_queries(image_owner, step_queries, devices, capacity)
    tokens, packed = lax.optimization_barrier((visual_tokens, packed))
    asked = lax.all_to_all(packed, "dp", split_axis=0, concat_axis=0, tiled=True)
    for_partner, ours = project(tokens, weight_half)
    from_partner = [lax.ppermute(piece, "tensor", [(0, 1), (1, 0)]) for piece in for_partner]

    cached = cached_attention(
        step_queries, cache_keys, cache_values, step_keys, step_values, cache_lengths
    )

    device = lax.axis_index("dp")
    own_lengths = lax.dynamic_index_in_dim(image_lengths, device, 0, keepdims=False)
    own_device = (
        lax.dynamic_slice_in_dim(image_owner, device * images_local, images_local) // rows_local
    )
    order = jnp.arange(images_local)
    earlier = order[None, :] < order[:, None]
    own_rank = jnp.sum(
        ((own_device[:, None] == own_device[None, :]) & earlier).astype(jnp.int32), axis=1
    )
    starts = jnp.sum(jnp.where(earlier, own_lengths[None, :], 0), axis=1)
    window_at = jnp.minimum(starts // 16 * 16, visual_tokens.shape[0] - VMAX - 16)
    places = jnp.stack([own_device * capacity + own_rank, window_at, starts - window_at, own_lengths])

    answers = visual_attention(places, asked, ours, from_partner)
    returned = lax.all_to_all(answers, "dp", split_axis=0, concat_axis=0, tiled=True)
    return merge(slot_of_row, returned, cached, rows_local)


def solution(mesh):
    return jax.shard_map(
        shards,
        mesh=mesh,
        in_specs=(
            P(("groups", "dp"), "tensor"),
            P("tensor", None, None, None),
            P("groups", None),
            P("groups"),
            P(("groups", "dp")),
            P(("groups", "dp"), None, "tensor"),
            P(("groups", "dp"), None, "tensor"),
            P(("groups", "dp"), None, "tensor"),
            P(("groups", "dp"), None, "tensor"),
            P(("groups", "dp"), None, "tensor"),
        ),
        out_specs=P(("groups", "dp"), None, "tensor"),
        check_vma=False,
    )
```

time: 66.1 us -> 48 us (0.73)
  local copies, waits for them, and re-layouts: 14.5 us -> 0.03 us
  Pallas kernels: 30 us -> 24.7 us
  starting transfers between devices: 11 us -> 14.4 us
  waiting for transfers between devices: 9 us -> 7.9 us
    unnamed x30 -> x8, local copies, waits for them, and re-layouts: 14.5 us -> 0.02 us
    pallas_call x5 -> x4, Pallas kernels: 26.2 us -> 18.5 us  [the longest x1 8.9 us: project(): pl.pallas_call(kernel, in_specs=[hbm, hbm], out_specs=[pl.BlockSpec(memor...]
    all_to_all x1, waiting for transfers between devices: 2.79 us -> 0.01 us  [shards(): lax.all_to_all(packed, 'dp', split_axis=0, concat_axis=0, tiled=True)]
    all_to_all x1, starting transfers between devices: 3.64 us -> 6.01 us  [shards(): lax.all_to_all(answers, 'dp', split_axis=0, concat_axis=0, tiled=True)]
    pallas_call x1, Pallas kernels: 3.82 us -> 6.17 us  [cached_attention(): pl.pallas_call(kernel, grid_spec=pltpu.PrefetchScalarGridSpec(num_scalar_...]
    ppermute x1 -> x4, waiting for transfers between devices: 0.01 us -> 1.57 us  [shards(): lax.ppermute(piece, 'tensor', [(0, 1), (1, 0)])]
  transfers between devices with their start and end apart: 3 -> 6, of which waited for: 2 -> 5; matrix products, arithmetic and copies ran while one was open for 1% -> 1% of each run, Pallas kernels for 33% -> 32%
where the time goes in v2:
time: 48 us; the launch traced here: 47.5 us
  Pallas kernels  24.7 us (51%)
  starting transfers between devices  14.4 us (30%)
  waiting for transfers between devices  7.9 us (16%)
  other arithmetic  0.5 us (1%)
    pallas_call x1, Pallas kernels, project(): pl.pallas_call(kernel, in_specs=[hbm, hbm], out_specs=[pl.BlockSpec(memor...  8.9 us
    all_to_all x1, starting transfers between devices, shards(): lax.all_to_all(packed, 'dp', split_axis=0, concat_axis=0, tiled=True)  7.29 us
    all_to_all x1, waiting for transfers between devices, shards(): lax.all_to_all(answers, 'dp', split_axis=0, concat_axis=0, tiled=True)  6.33 us
    pallas_call x1, Pallas kernels, cached_attention(): pl.pallas_call(kernel, grid_spec=pltpu.PrefetchScalarGridSpec(num_scalar_...  6.17 us
    all_to_all x1, starting transfers between devices, shards(): lax.all_to_all(answers, 'dp', split_axis=0, concat_axis=0, tiled=True)  6.01 us
    pallas_call x1, Pallas kernels, merge(): pl.pallas_call(kernel, in_specs=[pl.BlockSpec(memory_space=pltpu.SMEM), p...  3.58 us
    pallas_call x1, Pallas kernels, visual_attention(): pl.pallas_call(kernel, in_specs=[pl.BlockSpec(memory_space=pltpu.SMEM), p...  3.38 us
    pallas_call x1, Pallas kernels, pack_queries(): pl.pallas_call(kernel, in_specs=[pl.BlockSpec(memory_space=pl.ANY), pl.Bl...  2.62 us
  transfers between devices with their start and end apart: 6, of which 5 were waited for; matrix products, arithmetic and copies ran while one was open for 1% of the time, Pallas kernels for 32%

profile of v2, /device:TPU:0, one launch (start us, length us, event | category | flops | bytes accessed | tf_op | source)
XLA Modules:
  0.0 47.5 jit_solution(5556010335996256818)
XLA Ops:
  0.0 0.0 copy-start
  0.0 0.0 copy-start.3
  0.0 2.6 %pack_queries.1 = (bf16[24,4,2048]{2,1,0:T(4,128)(2,1)}, s32[25]{0:T(128)}) custom-call(s32[96]{0:T(128)} %owner_hbm.1, bf16[24,4,2048]{2,1,0:T(4,128)(2,1)} %q_ref.1), custom_call_target="tpu_custom_call" | custom-call | tf_op jit(solution)/shard_map/pack_queries/pallas_call | solution.py:65
  2.6 7.3 %all-to-all-start = ((bf16[24,4,2048]{2,1,0:T(4,128)(2,1)}), bf16[24,4,2048]{2,1,0:T(4,128)(2,1)S(1)}, u32[]{:S(2)}, u32[]{:S(2)}) async-start(bf16[24,4,2048]{2,1,0:T(4,128)(2,1)} %get-tuple-element.16), calls=%async_computation | async-start | bytes 786432 | tf_op jit(solution)/shard_map/all_to_all | solution.py:485
  9.9 8.9 %project.1 = (f32[120,640]{1,0:T(8,128)}, f32[120,640]{1,0:T(8,128)}, f32[120,640]{1,0:T(8,128)}, f32[120,640]{1,0:T(8,128)}, f32[16384,640]{1,0:T(8,128)}) custom-call(bf16[480,4096]{1,0:T(8,128)(2,1)} %token_hbm, bf16[4096,2,512]{2,1,0:T(2,128)(2,1)} %bitcast.18), custom_call_target="tpu_custom_call" | custom-call | flops 1048576 | bytes 65536 | tf_op jit(solution)/shard_map/project/pallas_call | solution.py:169
  18.8 0.1 collective-permute-start
  18.9 0.5 %collective-permute-start.1 = (f32[120,640]{1,0:T(8,128)}, f32[120,640]{1,0:T(8,128)S(1)}, u32[]{:S(2)}, u32[]{:S(2)}) collective-permute-start(f32[120,640]{1,0:T(8,128)} %get-tuple-element.20), channel_id=1, source_target_pairs={{0,1},{1,0},{2,3},{3,2},{4,5},{5,4},{6,7},{7,6},{8,9},{9,8},{10,11... | collective-permute-start | bytes 921608 | tf_op jit(solution)/shard_map/ppermute | solution.py:487
  19.4 0.1 collective-permute-start.2
  19.5 0.4 collective-permute-start.3
  19.9 0.0 copy-done
  19.9 0.1 select_reduce_fusion
  20.1 0.0 copy-done.3
  20.1 0.1 and_select_fusion.1
  20.1 0.2 convert_reduce_fusion
  20.4 0.1 add_bitcast_fusion
  20.5 0.3 collective-permute-done.refs_0_
  20.7 0.4 collective-permute-done.1.refs_1_
  21.2 0.4 collective-permute-done.2.refs_2_
  21.6 0.4 collective-permute-done.3.refs_3_
  22.0 0.0 all-to-all-done.q_ref
  22.0 3.4 %visual_attention.1 = bf16[24,4,2176]{2,1,0:T(4,128)(2,1)} custom-call(s32[4,12]{1,0:T(4,128)S(1)} %pad_add_fusion.place_ref, bf16[24,4,2048]{2,1,0:T(4,128)(2,1)S(1)} %all-to-all-done.q_ref, f32[16384,640]{1,0:T(8,128)} %get-tuple-element.18.ours_hbm, f32[120,640]{1,0:T(8,128)S(1)} %collective-permute-done.refs_0_, ...), custom_call_target="tpu_custom_call" | custom-call | tf_op jit(solution)/shard_map/visual_attention/pallas_call | solution.py:384
  25.4 6.0 %all-to-all-start.1 = ((bf16[24,4,2176]{2,1,0:T(4,128)(2,1)}), bf16[24,4,2176]{2,1,0:T(4,128)(2,1)S(1)}, u32[]{:S(2)}, u32[]{:S(2)}) async-start(bf16[24,4,2176]{2,1,0:T(4,128)(2,1)} %visual_attention.1), calls=%async_computation.1 | async-start | bytes 835584 | tf_op jit(solution)/shard_map/all_to_all | solution.py:508
  31.4 0.0 copy-start.2
  31.4 6.2 %cached_attention.1.cached_hbm = f32[1204,4,2176]{2,1,0:T(4,128)} custom-call(s32[24]{0:T(128)} %length_ref.1, bf16[24,4,2048]{2,1,0:T(4,128)(2,1)} %q_ref.1, bf16[24,128,256]{2,1,0:T(8,128)(2,1)} %k_ref.1, bf16[24,128,256]{2,1,0:T(8,128)(2,1)} %v_ref.1, bf16[24,4,256]{2,1,0:T(4,128)(2,1)} %sk_ref.1, bf16[24,4,256]{2,1,0:T(4,128)(2,1)} %sv_ref.1), custom_call_target="tpu_custom_call" | custom-call | flops 1048576 | bytes 65536 | tf_op jit(solution)/shard_map/cached_attention/pallas_call | solution.py:255
  37.6 6.3 %all-to-all-done.1.returned_ref = bf16[24,4,2176]{2,1,0:T(4,128)(2,1)S(1)} async-done(((bf16[24,4,2176]{2,1,0:T(4,128)(2,1)}), bf16[24,4,2176]{2,1,0:T(4,128)(2,1)S(1)}, u32[]{:S(2)}, u32[]{:S(2)}) %all-to-all-start.1) | async-done | bytes 417824 | tf_op jit(solution)/shard_map/all_to_all | solution.py:508
  43.9 0.0 copy-done.2
  43.9 0.0 copy-start.1
  43.9 3.6 %merge.1 = bf16[24,4,2048]{2,1,0:T(4,128)(2,1)} custom-call(s32[25]{0:T(128)S(1)} %copy-done.2, bf16[24,4,2176]{2,1,0:T(4,128)(2,1)S(1)} %all-to-all-done.1.returned_ref, f32[1204,4,2176]{2,1,0:T(4,128)} %cached_attention.1.cached_hbm), custom_call_target="tpu_custom_call" | custom-call | tf_op jit(solution)/shard_map/merge/pallas_call | solution.py:447
  47.5 0.0 copy-done.1
  (4 shorter events, 0.0 us)
Async XLA Ops:
  0.0 19.9 %copy-start = (s32[8,12]{1,0:T(8,128)S(1)}, s32[8,12]{1,0:T(8,128)}, u32[]{:S(2)}) copy-start(s32[8,12]{1,0:T(8,128)} %param.12) | copy-start | bytes 1156
  0.0 20.1 %copy-start.3 = (s32[96]{0:T(128)S(1)}, s32[96]{0:T(128)}, u32[]{:S(2)}) copy-start(s32[96]{0:T(128)} %owner_hbm.1) | copy-start | bytes 1156
  2.6 19.4 %all-to-all-start = ((bf16[24,4,2048]{2,1,0:T(4,128)(2,1)}), bf16[24,4,2048]{2,1,0:T(4,128)(2,1)S(1)}, u32[]{:S(2)}, u32[]{:S(2)}) async-start(bf16[24,4,2048]{2,1,0:T(4,128)(2,1)} %get-tuple-element.16), calls=%async_computation | async-start | bytes 786432 | tf_op jit(solution)/shard_map/all_to_all | solution.py:485
  18.8 1.9 %collective-permute-start = (f32[120,640]{1,0:T(8,128)}, f32[120,640]{1,0:T(8,128)S(1)}, u32[]{:S(2)}, u32[]{:S(2)}) collective-permute-start(f32[120,640]{1,0:T(8,128)} %get-tuple-element.19), channel_id=1, source_target_pairs={{0,1},{1,0},{2,3},{3,2},{4,5},{5,4},{6,7},{7,6},{8,9},{9,8},{10,11... | collective-permute-start | bytes 921608 | tf_op jit(solution)/shard_map/ppermute | solution.py:487
  18.9 2.2 %collective-permute-start.1 = (f32[120,640]{1,0:T(8,128)}, f32[120,640]{1,0:T(8,128)S(1)}, u32[]{:S(2)}, u32[]{:S(2)}) collective-permute-start(f32[120,640]{1,0:T(8,128)} %get-tuple-element.20), channel_id=1, source_target_pairs={{0,1},{1,0},{2,3},{3,2},{4,5},{5,4},{6,7},{7,6},{8,9},{9,8},{10,11... | collective-permute-start | bytes 921608 | tf_op jit(solution)/shard_map/ppermute | solution.py:487
  19.4 2.2 %collective-permute-start.2 = (f32[120,640]{1,0:T(8,128)}, f32[120,640]{1,0:T(8,128)S(1)}, u32[]{:S(2)}, u32[]{:S(2)}) collective-permute-start(f32[120,640]{1,0:T(8,128)} %get-tuple-element.21), channel_id=1, source_target_pairs={{0,1},{1,0},{2,3},{3,2},{4,5},{5,4},{6,7},{7,6},{8,9},{9,8},{10,11... | collective-permute-start | bytes 921608 | tf_op jit(solution)/shard_map/ppermute | solution.py:487
  19.5 2.5 %collective-permute-start.3 = (f32[120,640]{1,0:T(8,128)}, f32[120,640]{1,0:T(8,128)S(1)}, u32[]{:S(2)}, u32[]{:S(2)}) collective-permute-start(f32[120,640]{1,0:T(8,128)} %get-tuple-element.22), channel_id=1, source_target_pairs={{0,1},{1,0},{2,3},{3,2},{4,5},{5,4},{6,7},{7,6},{8,9},{9,8},{10,11... | collective-permute-start | bytes 921608 | tf_op jit(solution)/shard_map/ppermute | solution.py:487
  25.4 18.5 %all-to-all-start.1 = ((bf16[24,4,2176]{2,1,0:T(4,128)(2,1)}), bf16[24,4,2176]{2,1,0:T(4,128)(2,1)S(1)}, u32[]{:S(2)}, u32[]{:S(2)}) async-start(bf16[24,4,2176]{2,1,0:T(4,128)(2,1)} %visual_attention.1), calls=%async_computation.1 | async-start | bytes 835584 | tf_op jit(solution)/shard_map/all_to_all | solution.py:508
  31.4 12.5 %copy-start.2 = (s32[25]{0:T(128)S(1)}, s32[25]{0:T(128)}, u32[]{:S(2)}) copy-start(s32[25]{0:T(128)} %get-tuple-element.14.slot_ref) | copy-start | bytes 304
  43.9 3.6 %copy-start.1 = (s32[8,12]{1,0:T(8,128)S(1)}, s32[8,12]{1,0:T(8,128)}, u32[]{:S(2)}) copy-start(s32[8,12]{1,0:T(8,128)} %param.12) | copy-start | bytes 1156

commit v3 on v2

--- a/solution.py
+++ b/solution.py
@@ -12,7 +12,7 @@
 EPSILON = 1e-06
 LANES = 128
 FLOOR = -1e30
-PIECES = 4
+PIECES = 2
 FAR_BYTES = 40 << 20
 
 
@@ -22,14 +22,26 @@
 
 def dot(a, b):
     return jnp.dot(a, b, preferred_element_type=jnp.float32)
+
+
+def three_terms(value, lane, step):
+    first = value.astype(jnp.bfloat16).astype(jnp.float32)
+    rest = value - first
+    second = rest.astype(jnp.bfloat16).astype(jnp.float32)
+    third = jnp.where(lane < 3 * step, rest - second, 0.0)
+    terms = jnp.where(lane < step, first, jnp.where(lane < 2 * step, second, third))
+    return terms.astype(jnp.bfloat16)
 
 
 def pack_queries(image_owner, step_queries, devices, capacity):
     rows = step_queries.shape[0]
     images = image_owner.shape[0] // devices
     slots = devices * capacity
-
-    def kernel(owner_hbm, query_hbm, packed, slot_of_row, owner, queries, row_of_slot, in_sems, sems):
+    table = (rows // LANES + 1) * LANES
+
+    def kernel(
+        owner_hbm, query_hbm, packed, slot_out, owner, queries, row_of_slot, slot_of_row, in_sems, sems
+    ):
         read_owner = pltpu.make_async_copy(owner_hbm, owner, in_sems.at[0])
         read_queries = pltpu.make_async_copy(query_hbm, queries, in_sems.at[1])
         read_owner.start()
@@ -59,22 +71,26 @@
                 )
                 copy.start()
                 copies.append(copy)
+        write_slots = pltpu.make_async_copy(slot_of_row, slot_out, in_sems.at[2])
+        write_slots.start()
         for copy in copies:
             copy.wait()
+        write_slots.wait()
 
     return pl.pallas_call(
         kernel,
         in_specs=[pl.BlockSpec(memory_space=pl.ANY), pl.BlockSpec(memory_space=pl.ANY)],
-        out_specs=[pl.BlockSpec(memory_space=pl.ANY), pl.BlockSpec(memory_space=pltpu.SMEM)],
+        out_specs=[pl.BlockSpec(memory_space=pl.ANY), pl.BlockSpec(memory_space=pl.ANY)],
         out_shape=[
             jax.ShapeDtypeStruct((slots,) + step_queries.shape[1:], step_queries.dtype),
-            jax.ShapeDtypeStruct((rows + 1,), jnp.int32),
+            jax.ShapeDtypeStruct((table,), jnp.int32),
         ],
         scratch_shapes=[
             pltpu.SMEM(image_owner.shape, jnp.int32),
             pltpu.VMEM(step_queries.shape, step_queries.dtype),
             pltpu.SMEM((slots + 1,), jnp.int32),
-            pltpu.SemaphoreType.DMA((2,)),
+            pltpu.SMEM((table,), jnp.int32),
+            pltpu.SemaphoreType.DMA((3,)),
             pltpu.SemaphoreType.DMA((slots,)),
         ],
         name="pack_queries",
@@ -93,7 +109,7 @@
 
     def kernel(token_hbm, weight_hbm, *refs):
         pieces = refs[:PIECES]
-        ours_hbm, theirs_s, ours_s, token_s, weight_s, sems, out_sems = refs[PIECES:]
+        ours_hbm, ours_s, token_s, weight_s, sems, out_sem = refs[PIECES:]
         mine = lax.axis_index("tensor")
 
         def lanes(half):
@@ -112,14 +128,16 @@
                         token_hbm.at[:, span], token_s.at[:, span], sems.at[0, c]
                     ),
                     pltpu.make_async_copy(
-                        weight_hbm.at[span, :, lanes(1 - mine)],
-                        weight_s.at[0, span],
-                        sems.at[1, c],
+                        weight_hbm.at[span, :, lanes(mine)], weight_s.at[0, span], sems.at[1, c]
                     ),
                 ]
             )
         loads.append(
-            [pltpu.make_async_copy(weight_hbm.at[:, :, lanes(mine)], weight_s.at[1], sems.at[2, 0])]
+            [
+                pltpu.make_async_copy(
+                    weight_hbm.at[:, :, lanes(1 - mine)], weight_s.at[1], sems.at[2, 0]
+                )
+            ]
         )
 
         def start(c):
@@ -138,47 +156,40 @@
             x = token_s[:, span]
             part = product(x, weight_s[0, span])
             if c == 0:
-                theirs_s[:, : 2 * width] = part
+                ours_s[:, : 2 * width] = part
             else:
-                theirs_s[:, : 2 * width] += part
+                ours_s[:, : 2 * width] += part
             for lane in range(0, sizes[c], LANES):
                 wide = x[:, lane : lane + LANES].astype(jnp.float32)
                 squares += wide * wide
         squares = jnp.broadcast_to(jnp.sum(squares, axis=1, keepdims=True), (count, LANES))
-        theirs_s[:, 2 * width :] = squares
-        stores = []
-        for k in range(PIECES):
-            store = pltpu.make_async_copy(
-                theirs_s.at[pl.ds(k * piece, piece)], pieces[k], out_sems.at[k]
-            )
-            store.start()
-            stores.append(store)
         ours_s[:, 2 * width :] = squares
+        store = pltpu.make_async_copy(ours_s, ours_hbm.at[pl.ds(0, count)], out_sem)
+        store.start()
+        terms = three_terms(squares, lax.broadcasted_iota(jnp.int32, (count, LANES), 1), 1)
         for load in loads[chunks]:
             load.wait()
-        ours_s[:, : 2 * width] = product(token_s[...], weight_s[1])
-        store = pltpu.make_async_copy(
-            ours_s, ours_hbm.at[pl.ds(0, count)], out_sems.at[PIECES]
-        )
-        store.start()
-        stores.append(store)
-        for store in stores:
-            store.wait()
+        theirs = product(token_s[...], weight_s[1]).astype(jnp.bfloat16)
+        for k, piece_ref in enumerate(pieces):
+            span = slice(k * piece, (k + 1) * piece)
+            piece_ref[:, : 2 * width] = theirs[span]
+            piece_ref[:, 2 * width :] = terms[span]
+        store.wait()
 
     hbm = pl.BlockSpec(memory_space=pltpu.HBM)
     *theirs, ours = pl.pallas_call(
         kernel,
         in_specs=[hbm, hbm],
-        out_specs=[pl.BlockSpec(memory_space=pl.ANY)] * (PIECES + 1),
-        out_shape=[jax.ShapeDtypeStruct((piece, columns), jnp.float32)] * PIECES
+        out_specs=[pl.BlockSpec(memory_space=pltpu.VMEM)] * PIECES
+        + [pl.BlockSpec(memory_space=pl.ANY)],
+        out_shape=[jax.ShapeDtypeStruct((piece, columns), jnp.bfloat16)] * PIECES
         + [jax.ShapeDtypeStruct((FAR_BYTES // (4 * columns), columns), jnp.float32)],
         scratch_shapes=[
-            pltpu.VMEM((count, columns), jnp.float32),
             pltpu.VMEM((count, columns), jnp.float32),
             pltpu.VMEM(tokens.shape, tokens.dtype),
             pltpu.VMEM((2, depth, 2, width), weight.dtype),
             pltpu.SemaphoreType.DMA((3, chunks)),
-            pltpu.SemaphoreType.DMA((PIECES + 1,)),
+            pltpu.SemaphoreType.DMA,
         ],
         compiler_params=pltpu.CompilerParams(vmem_limit_bytes=60 << 20),
         cost_estimate=pl.CostEstimate(flops=1 << 20, bytes_accessed=1 << 16, transcendentals=0),
@@ -283,7 +294,7 @@
 
 
 def visual_attention(places, queries, ours, received):
-    images = places.shape[1]
+    images = places.shape[0] // 4
     slots, _, full = queries.shape
     heads = full // HD
     columns = ours.shape[1]
@@ -296,11 +307,14 @@
     window = VMAX + 16
     scale = HD**-0.5
 
-    def kernel(place_ref, q_ref, ours_hbm, *refs):
+    def kernel(place_hbm, q_ref, ours_hbm, *refs):
         received_hbm = refs[:PIECES]
-        out_hbm, ours_s, received_s, pair_ref, q_s, score_s, weight_s, out_ref, load_sems, sems = refs[
-            PIECES:
+        out_hbm, place_ref, ours_s, received_s, pair_ref, q_s, score_s, weight_s, out_ref = refs[
+            PIECES:-3
         ]
+        place_sem, load_sems, sems = refs[-3:]
+        read_places = pltpu.make_async_copy(place_hbm, place_ref, place_sem)
+        read_places.start()
         loads = []
         for k in range(PIECES):
             rows = pl.ds(k * piece, piece)
@@ -312,8 +326,9 @@
                 load.start()
             loads.append(pair)
         stores = []
+        read_places.wait()
         for i in range(images):
-            slot = place_ref[0, i]
+            slot = place_ref[0 * images + i]
             for h in range(heads):
                 q_s[i, h * STEPS : (h + 1) * STEPS, :] = q_ref[
                     slot, :, h * HD : (h + 1) * HD
@@ -322,13 +337,16 @@
             for load in loads[k]:
                 load.wait()
             rows = slice(k * piece, (k + 1) * piece)
-            factor = lax.rsqrt((ours_s[rows, split:] + received_s[rows, split:]) / D + EPSILON)
+            squares = jnp.sum(
+                received_s[rows, split:].astype(jnp.float32), axis=1, keepdims=True
+            )
+            factor = lax.rsqrt((ours_s[rows, split:] + squares) / D + EPSILON)
             for at in range(0, split, LANES):
                 lanes = slice(at, at + LANES)
-                total = (ours_s[rows, lanes] + received_s[rows, lanes]) * factor
+                total = (ours_s[rows, lanes] + received_s[rows, lanes].astype(jnp.float32)) * factor
                 pair_ref[rows, lanes] = total.astype(pair_ref.dtype)
         for i in range(images):
-            rows = pl.ds(pl.multiple_of(place_ref[1, i], 16), window)
+            rows = pl.ds(pl.multiple_of(place_ref[1 * images + i], 16), window)
             q = q_s[i].astype(jnp.bfloat16)
             for g in range(kv_local):
                 score_s[i, g * stacked : (g + 1) * stacked, :] = dot_t(
@@ -338,8 +356,8 @@
         inverses = []
         logs = []
         for i in range(images):
-            start = place_ref[2, i]
-            live = (column >= start) & (column < start + place_ref[3, i])
+            start = place_ref[2 * images + i]
+            live = (column >= start) & (column < start + place_ref[3 * images + i])
             scores = jnp.where(live, score_s[i] * scale, FLOOR)
             peak = jnp.max(scores, axis=1, keepdims=True)
             weights = jnp.exp(scores - peak)
@@ -349,7 +367,7 @@
             logs.append(jnp.broadcast_to(peak + jnp.log(total), (heads * STEPS, LANES)))
         lane = lax.broadcasted_iota(jnp.int32, (STEPS, LANES), 1)
         for i in range(images):
-            rows = pl.ds(pl.multiple_of(place_ref[1, i], 16), window)
+            rows = pl.ds(pl.multiple_of(place_ref[1 * images + i], 16), window)
             for g in range(kv_local):
                 at = (kv_local + g) * HD
                 part = dot(
@@ -365,16 +383,8 @@
             for h in range(heads):
                 log = logs[i][h * STEPS : (h + 1) * STEPS]
                 packed = jnp.where(lane % heads == h, log, packed)
-            first = packed.astype(jnp.bfloat16).astype(jnp.float32)
-            rest = packed - first
-            second = rest.astype(jnp.bfloat16).astype(jnp.float32)
-            third = rest - second
-            out_ref[i, :, full:] = jnp.where(
-                lane < heads,
-                first,
-                jnp.where(lane < 2 * heads, second, jnp.where(lane < 3 * heads, third, 0.0)),
-            ).astype(out_ref.dtype)
-            store = pltpu.make_async_copy(out_ref.at[i], out_hbm.at[place_ref[0, i]], sems.at[i])
+            out_ref[i, :, full:] = three_terms(packed, lane, heads)
+            store = pltpu.make_async_copy(out_ref.at[i], out_hbm.at[place_ref[0 * images + i]], sems.at[i])
             store.start()
             stores.append(store)
         for store in stores:
@@ -384,20 +394,22 @@
     return pl.pallas_call(
         kernel,
         in_specs=[
-            pl.BlockSpec(memory_space=pltpu.SMEM),
+            anywhere,
             pl.BlockSpec(memory_space=pltpu.VMEM),
         ]
         + [anywhere] * (1 + PIECES),
         out_specs=anywhere,
         out_shape=jax.ShapeDtypeStruct((slots, STEPS, full + LANES), queries.dtype),
         scratch_shapes=[
+            pltpu.SMEM(places.shape, jnp.int32),
             pltpu.VMEM((count, columns), jnp.float32),
-            pltpu.VMEM((count, columns), jnp.float32),
+            pltpu.VMEM((count, columns), jnp.bfloat16),
             pltpu.VMEM((count, split), jnp.bfloat16),
             pltpu.VMEM((images, heads * STEPS, HD), jnp.float32),
             pltpu.VMEM((images, heads * STEPS, window), jnp.float32),
             pltpu.VMEM((images, heads * STEPS, window), jnp.bfloat16),
             pltpu.VMEM((images, STEPS, full + LANES), queries.dtype),
+            pltpu.SemaphoreType.DMA,
             pltpu.SemaphoreType.DMA((2, PIECES)),
             pltpu.SemaphoreType.DMA((images,)),
         ],
@@ -412,7 +424,9 @@
     runs = 3 if rows % 3 == 0 else 1
     run = rows // runs
 
-    def kernel(slot_ref, returned_ref, cached_hbm, out_hbm, cached_s, out_s, sems):
+    def kernel(slot_hbm, returned_ref, cached_hbm, out_hbm, slot_ref, cached_s, out_s, slot_sem, sems):
+        read_slots = pltpu.make_async_copy(slot_hbm, slot_ref, slot_sem)
+        read_slots.start()
         loads = []
         stores = []
         for k in range(runs):
@@ -420,6 +434,7 @@
             load = pltpu.make_async_copy(cached_hbm.at[span], cached_s.at[span], sems.at[0, k])
             load.start()
             loads.append(load)
+        read_slots.wait()
         for k in range(runs):
             loads[k].wait()
             for r in range(k * run, (k + 1) * run):
@@ -447,15 +462,17 @@
     return pl.pallas_call(
         kernel,
         in_specs=[
-            pl.BlockSpec(memory_space=pltpu.SMEM),
+            anywhere,
             pl.BlockSpec(memory_space=pltpu.VMEM),
             anywhere,
         ],
         out_specs=anywhere,
         out_shape=jax.ShapeDtypeStruct((rows, STEPS, full), jnp.bfloat16),
         scratch_shapes=[
+            pltpu.SMEM(slot_of_row.shape, jnp.int32),
             pltpu.VMEM((rows, STEPS, full + LANES), jnp.float32),
             pltpu.VMEM((rows, STEPS, full), jnp.bfloat16),
+            pltpu.SemaphoreType.DMA,
             pltpu.SemaphoreType.DMA((2, runs)),
         ],
         compiler_params=pltpu.CompilerParams(vmem_limit_bytes=32 << 20),
@@ -502,7 +519,9 @@
     )
     starts = jnp.sum(jnp.where(earlier, own_lengths[None, :], 0), axis=1)
     window_at = jnp.minimum(starts // 16 * 16, visual_tokens.shape[0] - VMAX - 16)
-    places = jnp.stack([own_device * capacity + own_rank, window_at, starts - window_at, own_lengths])
+    places = jnp.concatenate(
+        [own_device * capacity + own_rank, window_at, starts - window_at, own_lengths]
+    )
 
     answers = visual_attention(places, asked, ours, from_partner)
     returned = lax.all_to_all(answers, "dp", split_axis=0, concat_axis=0, tiled=True)

time: 48 us -> 45.3 us (0.944)
  Pallas kernels: 24.7 us -> 22.9 us
  starting transfers between devices: 14.4 us -> 13.2 us
    pallas_call x2, Pallas kernels: 6.97 us -> 5.93 us  [the longest x1 3.07 us: merge(): pl.pallas_call(kernel, in_specs=[anywhere, pl.BlockSpec(memory_space=pltp...]
    all_to_all x1, waiting for transfers between devices: 0.01 us -> 0.7 us  [shards(): lax.all_to_all(packed, 'dp', split_axis=0, concat_axis=0, tiled=True)]
    all_to_all x1, starting transfers between devices: 6.01 us -> 5.32 us  [shards(): lax.all_to_all(answers, 'dp', split_axis=0, concat_axis=0, tiled=True)]
    ppermute x4 -> x2, starting transfers between devices: 1.08 us -> 0.57 us  [shards(): lax.ppermute(piece, 'tensor', [(0, 1), (1, 0)])]
    pallas_call x1, Pallas kernels: 2.62 us -> 2.13 us  [pack_queries(): pl.pallas_call(kernel, in_specs=[pl.BlockSpec(memory_space=pl.ANY), pl.Bl...]
    ppermute x4 -> x2, waiting for transfers between devices: 1.57 us -> 1.15 us  [shards(): lax.ppermute(piece, 'tensor', [(0, 1), (1, 0)])]
  transfers between devices with their start and end apart: 6 -> 4, of which waited for: 5 -> 4; matrix products, arithmetic and copies ran while one was open for 1% -> 1% of each run, Pallas kernels for 32% -> 33%
where the time goes in v3:
time: 45.3 us; the launch traced here: 44.9 us
  Pallas kernels  22.9 us (51%)
  starting transfers between devices  13.2 us (29%)
  waiting for transfers between devices  8.17 us (18%)
  other arithmetic  0.57 us (1%)
    pallas_call x1, Pallas kernels, project(): pl.pallas_call(kernel, in_specs=[hbm, hbm], out_specs=[pl.BlockSpec(memor...  8.66 us
    all_to_all x1, starting transfers between devices, shards(): lax.all_to_all(packed, 'dp', split_axis=0, concat_axis=0, tiled=True)  7.29 us
    all_to_all x1, waiting for transfers between devices, shards(): lax.all_to_all(answers, 'dp', split_axis=0, concat_axis=0, tiled=True)  6.32 us
    pallas_call x1, Pallas kernels, cached_attention(): pl.pallas_call(kernel, grid_spec=pltpu.PrefetchScalarGridSpec(num_scalar_...  6.18 us
    all_to_all x1, starting transfers between devices, shards(): lax.all_to_all(answers, 'dp', split_axis=0, concat_axis=0, tiled=True)  5.32 us
    pallas_call x1, Pallas kernels, merge(): pl.pallas_call(kernel, in_specs=[anywhere, pl.BlockSpec(memory_space=pltp...  3.07 us
    pallas_call x1, Pallas kernels, visual_attention(): pl.pallas_call(kernel, in_specs=[anywhere, pl.BlockSpec(memory_space=pltp...  2.86 us
    pallas_call x1, Pallas kernels, pack_queries(): pl.pallas_call(kernel, in_specs=[pl.BlockSpec(memory_space=pl.ANY), pl.Bl...  2.13 us
  transfers between devices with their start and end apart: 4, of which 4 were waited for; matrix products, arithmetic and copies ran while one was open for 1% of the time, Pallas kernels for 33%

profile of v3, /device:TPU:0, one launch (start us, length us, event | category | flops | bytes accessed | tf_op | source)
XLA Modules:
  0.0 44.9 jit_solution(5411259408242125896)
XLA Ops:
  0.0 0.0 copy-start
  0.0 0.0 copy-start.3
  0.0 2.1 %pack_queries.1 = (bf16[24,4,2048]{2,1,0:T(4,128)(2,1)}, s32[128]{0:T(128)}) custom-call(s32[96]{0:T(128)} %owner_hbm.1, bf16[24,4,2048]{2,1,0:T(4,128)(2,1)} %q_ref.1), custom_call_target="tpu_custom_call" | custom-call | tf_op jit(solution)/shard_map/pack_queries/pallas_call | solution.py:80
  2.1 7.3 %all-to-all-start = ((bf16[24,4,2048]{2,1,0:T(4,128)(2,1)}), bf16[24,4,2048]{2,1,0:T(4,128)(2,1)S(1)}, u32[]{:S(2)}, u32[]{:S(2)}) async-start(bf16[24,4,2048]{2,1,0:T(4,128)(2,1)} %get-tuple-element.14), calls=%async_computation | async-start | bytes 786432 | tf_op jit(solution)/shard_map/all_to_all | solution.py:502
  9.4 8.7 %project.1 = (bf16[240,640]{1,0:T(8,128)(2,1)}, bf16[240,640]{1,0:T(8,128)(2,1)}, f32[16384,640]{1,0:T(8,128)}) custom-call(bf16[480,4096]{1,0:T(8,128)(2,1)} %token_hbm, bf16[4096,2,512]{2,1,0:T(2,128)(2,1)} %bitcast.3), custom_call_target="tpu_custom_call" | custom-call | flops 1048576 | bytes 65536 | tf_op jit(solution)/shard_map/project/pallas_call | solution.py:180
  18.1 0.1 collective-permute-start
  18.2 0.5 %collective-permute-start.1 = (bf16[240,640]{1,0:T(8,128)(2,1)}, bf16[240,640]{1,0:T(8,128)(2,1)S(1)}, u32[]{:S(2)}, u32[]{:S(2)}) collective-permute-start(bf16[240,640]{1,0:T(8,128)(2,1)} %get-tuple-element.18), channel_id=1, source_target_pairs={{0,1},{1,0},{2,3},{3,2},{4,5},{5,4},{6,7},{7,6},{8,9},{9,8},{10,11... | collective-permute-start | bytes 921608 | tf_op jit(solution)/shard_map/ppermute | solution.py:504
  18.7 0.0 copy-done
  18.7 0.1 select_reduce_fusion
  18.8 0.0 copy-done.3
  18.8 0.1 and_select_fusion.1
  18.9 0.2 convert_reduce_fusion
  19.1 0.1 multiply_add_fusion
  19.2 0.1 pad_add_fusion.place_hbm
  19.3 0.7 %collective-permute-done.refs_0_ = bf16[240,640]{1,0:T(8,128)(2,1)S(1)} collective-permute-done((bf16[240,640]{1,0:T(8,128)(2,1)}, bf16[240,640]{1,0:T(8,128)(2,1)S(1)}, u32[]{:S(2)}, u32[]{:S(2)}) %collective-permute-start) | collective-permute-done | bytes 307232 | tf_op jit(solution)/shard_map/ppermute | solution.py:504
  20.0 0.4 collective-permute-done.1.refs_1_
  20.4 0.7 %all-to-all-done.q_ref = bf16[24,4,2048]{2,1,0:T(4,128)(2,1)S(1)} async-done(((bf16[24,4,2048]{2,1,0:T(4,128)(2,1)}), bf16[24,4,2048]{2,1,0:T(4,128)(2,1)S(1)}, u32[]{:S(2)}, u32[]{:S(2)}) %all-to-all-start) | async-done | bytes 393248 | tf_op jit(solution)/shard_map/all_to_all | solution.py:502
  21.1 2.9 %visual_attention.1 = bf16[24,4,2176]{2,1,0:T(4,128)(2,1)} custom-call(s32[48]{0:T(128)S(1)} %pad_add_fusion.place_hbm, bf16[24,4,2048]{2,1,0:T(4,128)(2,1)S(1)} %all-to-all-done.q_ref, f32[16384,640]{1,0:T(8,128)} %get-tuple-element.16.ours_hbm, bf16[240,640]{1,0:T(8,128)(2,1)S(1)} %collective-permute-done.refs_0_, ...), custom_call_target="tpu_custom_call" | custom-call | tf_op jit(solution)/shard_map/visual_attention/pallas_call | solution.py:394
  24.0 5.3 %all-to-all-start.1 = ((bf16[24,4,2176]{2,1,0:T(4,128)(2,1)}), bf16[24,4,2176]{2,1,0:T(4,128)(2,1)S(1)}, u32[]{:S(2)}, u32[]{:S(2)}) async-start(bf16[24,4,2176]{2,1,0:T(4,128)(2,1)} %visual_attention.1), calls=%async_computation.1 | async-start | bytes 835584 | tf_op jit(solution)/shard_map/all_to_all | solution.py:527
  29.3 0.0 copy-start.2
  29.3 6.2 %cached_attention.1.cached_hbm = f32[1204,4,2176]{2,1,0:T(4,128)} custom-call(s32[24]{0:T(128)} %length_ref.1, bf16[24,4,2048]{2,1,0:T(4,128)(2,1)} %q_ref.1, bf16[24,128,256]{2,1,0:T(8,128)(2,1)} %k_ref.1, bf16[24,128,256]{2,1,0:T(8,128)(2,1)} %v_ref.1, bf16[24,4,256]{2,1,0:T(4,128)(2,1)} %sk_ref.1, bf16[24,4,256]{2,1,0:T(4,128)(2,1)} %sv_ref.1), custom_call_target="tpu_custom_call" | custom-call | flops 1048576 | bytes 65536 | tf_op jit(solution)/shard_map/cached_attention/pallas_call | solution.py:266
  35.5 6.3 %all-to-all-done.1.returned_ref = bf16[24,4,2176]{2,1,0:T(4,128)(2,1)S(1)} async-done(((bf16[24,4,2176]{2,1,0:T(4,128)(2,1)}), bf16[24,4,2176]{2,1,0:T(4,128)(2,1)S(1)}, u32[]{:S(2)}, u32[]{:S(2)}) %all-to-all-start.1) | async-done | bytes 417824 | tf_op jit(solution)/shard_map/all_to_all | solution.py:527
  41.8 0.0 copy-done.2
  41.8 0.0 copy-start.1
  41.8 3.1 %merge.1 = bf16[24,4,2048]{2,1,0:T(4,128)(2,1)} custom-call(s32[128]{0:T(128)S(1)} %copy-done.2, bf16[24,4,2176]{2,1,0:T(4,128)(2,1)S(1)} %all-to-all-done.1.returned_ref, f32[1204,4,2176]{2,1,0:T(4,128)} %cached_attention.1.cached_hbm), custom_call_target="tpu_custom_call" | custom-call | tf_op jit(solution)/shard_map/merge/pallas_call | solution.py:462
  44.9 0.0 copy-done.1
  (2 shorter events, 0.0 us)
Async XLA Ops:
  0.0 18.7 %copy-start = (s32[8,12]{1,0:T(8,128)S(1)}, s32[8,12]{1,0:T(8,128)}, u32[]{:S(2)}) copy-start(s32[8,12]{1,0:T(8,128)} %param.12) | copy-start | bytes 1156
  0.0 18.8 %copy-start.3 = (s32[96]{0:T(128)S(1)}, s32[96]{0:T(128)}, u32[]{:S(2)}) copy-start(s32[96]{0:T(128)} %owner_hbm.1) | copy-start | bytes 1156
  2.1 19.0 %all-to-all-start = ((bf16[24,4,2048]{2,1,0:T(4,128)(2,1)}), bf16[24,4,2048]{2,1,0:T(4,128)(2,1)S(1)}, u32[]{:S(2)}, u32[]{:S(2)}) async-start(bf16[24,4,2048]{2,1,0:T(4,128)(2,1)} %get-tuple-element.14), calls=%async_computation | async-start | bytes 786432 | tf_op jit(solution)/shard_map/all_to_all | solution.py:502
  18.1 1.9 %collective-permute-start = (bf16[240,640]{1,0:T(8,128)(2,1)}, bf16[240,640]{1,0:T(8,128)(2,1)S(1)}, u32[]{:S(2)}, u32[]{:S(2)}) collective-permute-start(bf16[240,640]{1,0:T(8,128)(2,1)} %get-tuple-element.17), channel_id=1, source_target_pairs={{0,1},{1,0},{2,3},{3,2},{4,5},{5,4},{6,7},{7,6},{8,9},{9,8},{10,11... | collective-permute-start | bytes 921608 | tf_op jit(solution)/shard_map/ppermute | solution.py:504
  18.2 2.2 %collective-permute-start.1 = (bf16[240,640]{1,0:T(8,128)(2,1)}, bf16[240,640]{1,0:T(8,128)(2,1)S(1)}, u32[]{:S(2)}, u32[]{:S(2)}) collective-permute-start(bf16[240,640]{1,0:T(8,128)(2,1)} %get-tuple-element.18), channel_id=1, source_target_pairs={{0,1},{1,0},{2,3},{3,2},{4,5},{5,4},{6,7},{7,6},{8,9},{9,8},{10,11... | collective-permute-start | bytes 921608 | tf_op jit(solution)/shard_map/ppermute | solution.py:504
  24.0 17.8 %all-to-all-start.1 = ((bf16[24,4,2176]{2,1,0:T(4,128)(2,1)}), bf16[24,4,2176]{2,1,0:T(4,128)(2,1)S(1)}, u32[]{:S(2)}, u32[]{:S(2)}) async-start(bf16[24,4,2176]{2,1,0:T(4,128)(2,1)} %visual_attention.1), calls=%async_computation.1 | async-start | bytes 835584 | tf_op jit(solution)/shard_map/all_to_all | solution.py:527
  29.3 12.5 %copy-start.2 = (s32[128]{0:T(128)S(1)}, s32[128]{0:T(128)}, u32[]{:S(2)}) copy-start(s32[128]{0:T(128)} %get-tuple-element.12.slot_hbm) | copy-start | bytes 1540
  41.8 3.1 %copy-start.1 = (s32[8,12]{1,0:T(8,128)S(1)}, s32[8,12]{1,0:T(8,128)}, u32[]{:S(2)}) copy-start(s32[8,12]{1,0:T(8,128)} %param.12) | copy-start | bytes 1156

commit v4 on v3

--- a/solution.py
+++ b/solution.py
@@ -12,8 +12,24 @@
 EPSILON = 1e-06
 LANES = 128
 FLOOR = -1e30
-PIECES = 2
-FAR_BYTES = 40 << 20
+RUNS = 4
+ORDERS = {8: (5, 6, 4, 3, 1, 7, 2, 0)}
+FAR_BYTES = 36 << 20
+
+
+def exchange_order(devices):
+    return ORDERS.get(devices, tuple(range(devices)))
+
+
+def exchange(slots, devices):
+    return lax.all_to_all(
+        slots,
+        "dp",
+        split_axis=0,
+        concat_axis=0,
+        tiled=True,
+        axis_index_groups=[list(exchange_order(devices))],
+    )
 
 
 def dot_t(a, b):
@@ -53,19 +69,19 @@
             row_of_slot[slot] = 0
         read_owner.wait()
         copies = []
-        for s in range(devices):
+        for place, s in enumerate(exchange_order(devices)):
             rank = jnp.int32(0)
             for i in range(images):
                 row = owner[s * images + i] - base
                 local = jnp.logical_and(row >= 0, row < rows)
-                slot = s * capacity + rank
+                slot = place * capacity + rank
                 row_of_slot[jnp.where(local, slot, slots)] = row
                 slot_of_row[jnp.where(local, row, rows)] = slot
                 rank = rank + local.astype(jnp.int32)
-            if s == 0:
+            if place == 0:
                 read_queries.wait()
             for k in range(capacity):
-                slot = s * capacity + k
+                slot = place * capacity + k
                 copy = pltpu.make_async_copy(
                     queries.at[row_of_slot[slot]], packed.at[slot], sems.at[slot]
                 )
@@ -101,15 +117,14 @@
     count, depth = tokens.shape
     width = weight.shape[2] // 2
     columns = 2 * width + LANES
-    piece = count // PIECES
     sizes = [512, 512] + [1024] * ((depth - 1024) // 1024)
     starts = [sum(sizes[:c]) for c in range(len(sizes))]
     chunks = len(sizes)
     ahead = 3
 
-    def kernel(token_hbm, weight_hbm, *refs):
-        pieces = refs[:PIECES]
-        ours_hbm, ours_s, token_s, weight_s, sems, out_sem = refs[PIECES:]
+    def kernel(
+        token_hbm, weight_hbm, theirs_ref, ours_hbm, ours_s, token_s, weight_s, sems, out_sem
+    ):
         mine = lax.axis_index("tensor")
 
         def lanes(half):
@@ -169,21 +184,19 @@
         terms = three_terms(squares, lax.broadcasted_iota(jnp.int32, (count, LANES), 1), 1)
         for load in loads[chunks]:
             load.wait()
-        theirs = product(token_s[...], weight_s[1]).astype(jnp.bfloat16)
-        for k, piece_ref in enumerate(pieces):
-            span = slice(k * piece, (k + 1) * piece)
-            piece_ref[:, : 2 * width] = theirs[span]
-            piece_ref[:, 2 * width :] = terms[span]
+        theirs_ref[:, : 2 * width] = product(token_s[...], weight_s[1]).astype(jnp.bfloat16)
+        theirs_ref[:, 2 * width :] = terms
         store.wait()
 
     hbm = pl.BlockSpec(memory_space=pltpu.HBM)
-    *theirs, ours = pl.pallas_call(
+    return pl.pallas_call(
         kernel,
         in_specs=[hbm, hbm],
-        out_specs=[pl.BlockSpec(memory_space=pltpu.VMEM)] * PIECES
-        + [pl.BlockSpec(memory_space=pl.ANY)],
-        out_shape=[jax.ShapeDtypeStruct((piece, columns), jnp.bfloat16)] * PIECES
-        + [jax.ShapeDtypeStruct((FAR_BYTES // (4 * columns), columns), jnp.float32)],
+        out_specs=[pl.BlockSpec(memory_space=pltpu.VMEM), pl.BlockSpec(memory_space=pl.ANY)],
+        out_shape=[
+            jax.ShapeDtypeStruct((count, columns), jnp.bfloat16),
+            jax.ShapeDtypeStruct((FAR_BYTES // (4 * columns), columns), jnp.float32),
+        ],
         scratch_shapes=[
             pltpu.VMEM((count, columns), jnp.float32),
             pltpu.VMEM(tokens.shape, tokens.dtype),
@@ -195,7 +208,6 @@
         cost_estimate=pl.CostEstimate(flops=1 << 20, bytes_accessed=1 << 16, transcendentals=0),
         name="project",
     )(tokens, weight)
-    return theirs, ours
 
 
 def cached_attention(queries, cache_keys, cache_values, step_keys, step_values, lengths):
@@ -254,11 +266,11 @@
                 for j in range(group):
                     h = g * group + j
                     head = slice(j * STEPS, (j + 1) * STEPS)
-                    out_ref[r, :, h * HD : (h + 1) * HD] = part[head]
+                    out_ref[r * STEPS : (r + 1) * STEPS, h * HD : (h + 1) * HD] = part[head]
                     at = r * stacked + j * STEPS
                     logs[r] = jnp.where(lane == h, log[at : at + STEPS], logs[r])
         for r in range(block):
-            out_ref[r, :, heads * HD :] = logs[r]
+            out_ref[r * STEPS : (r + 1) * STEPS, heads * HD :] = logs[r]
 
     def spec(array):
         return pl.BlockSpec((block,) + array.shape[1:], lambda i, length_ref: (i, 0, 0))
@@ -276,7 +288,7 @@
                 spec(step_values),
             ],
             out_specs=pl.BlockSpec(
-                (block, STEPS, heads * HD + LANES), lambda i, length_ref: (i, 0, 0)
+                (block * STEPS, heads * HD + LANES), lambda i, length_ref: (i, 0)
             ),
             scratch_shapes=[
                 pltpu.VMEM((kv_local, block * stacked, HD), jnp.float32),
@@ -285,7 +297,7 @@
             ],
         ),
         out_shape=jax.ShapeDtypeStruct(
-            (FAR_BYTES // (4 * STEPS * (heads * HD + LANES)), STEPS, heads * HD + LANES), jnp.float32
+            (FAR_BYTES // (4 * (heads * HD + LANES)), heads * HD + LANES), jnp.float32
         ),
         compiler_params=pltpu.CompilerParams(vmem_limit_bytes=60 << 20),
         cost_estimate=pl.CostEstimate(flops=1 << 20, bytes_accessed=1 << 16, transcendentals=0),
@@ -300,31 +312,38 @@
     columns = ours.shape[1]
     split = columns - LANES
     kv_local = split // (2 * HD)
-    piece = received[0].shape[0]
-    count = piece * PIECES
+    count = received.shape[0]
+    run = count // RUNS
     group = heads // kv_local
     stacked = group * STEPS
     window = VMAX + 16
     scale = HD**-0.5
 
-    def kernel(place_hbm, q_ref, ours_hbm, *refs):
-        received_hbm = refs[:PIECES]
-        out_hbm, place_ref, ours_s, received_s, pair_ref, q_s, score_s, weight_s, out_ref = refs[
-            PIECES:-3
-        ]
-        place_sem, load_sems, sems = refs[-3:]
+    def kernel(
+        place_hbm,
+        q_ref,
+        received_ref,
+        ours_hbm,
+        out_hbm,
+        place_ref,
+        ours_s,
+        pair_ref,
+        q_s,
+        score_s,
+        weight_s,
+        out_ref,
+        place_sem,
+        load_sems,
+        sems,
+    ):
         read_places = pltpu.make_async_copy(place_hbm, place_ref, place_sem)
         read_places.start()
         loads = []
-        for k in range(PIECES):
-            rows = pl.ds(k * piece, piece)
-            pair = (
-                pltpu.make_async_copy(ours_hbm.at[rows], ours_s.at[rows], load_sems.at[0, k]),
-                pltpu.make_async_copy(received_hbm[k], received_s.at[rows], load_sems.at[1, k]),
-            )
-            for load in pair:
-                load.start()
-            loads.append(pair)
+        for k in range(RUNS):
+            rows = pl.ds(k * run, run)
+            load = pltpu.make_async_copy(ours_hbm.at[rows], ours_s.at[rows], load_sems.at[k])
+            load.start()
+            loads.append(load)
         stores = []
         read_places.wait()
         for i in range(images):
@@ -333,17 +352,16 @@
                 q_s[i, h * STEPS : (h + 1) * STEPS, :] = q_ref[
                     slot, :, h * HD : (h + 1) * HD
                 ].astype(jnp.float32)
-        for k in range(PIECES):
-            for load in loads[k]:
-                load.wait()
-            rows = slice(k * piece, (k + 1) * piece)
+        for k in range(RUNS):
+            loads[k].wait()
+            rows = slice(k * run, (k + 1) * run)
             squares = jnp.sum(
-                received_s[rows, split:].astype(jnp.float32), axis=1, keepdims=True
+                received_ref[rows, split:].astype(jnp.float32), axis=1, keepdims=True
             )
             factor = lax.rsqrt((ours_s[rows, split:] + squares) / D + EPSILON)
             for at in range(0, split, LANES):
                 lanes = slice(at, at + LANES)
-                total = (ours_s[rows, lanes] + received_s[rows, lanes].astype(jnp.float32)) * factor
+                total = (ours_s[rows, lanes] + received_ref[rows, lanes].astype(jnp.float32)) * factor
                 pair_ref[rows, lanes] = total.astype(pair_ref.dtype)
         for i in range(images):
             rows = pl.ds(pl.multiple_of(place_ref[1 * images + i], 16), window)
@@ -391,67 +409,77 @@
             store.wait()
 
     anywhere = pl.BlockSpec(memory_space=pl.ANY)
+    vmem = pl.BlockSpec(memory_space=pltpu.VMEM)
     return pl.pallas_call(
         kernel,
         in_specs=[
             anywhere,
-            pl.BlockSpec(memory_space=pltpu.VMEM),
-        ]
-        + [anywhere] * (1 + PIECES),
+            vmem,
+            vmem,
+            anywhere,
+        ],
         out_specs=anywhere,
         out_shape=jax.ShapeDtypeStruct((slots, STEPS, full + LANES), queries.dtype),
         scratch_shapes=[
             pltpu.SMEM(places.shape, jnp.int32),
             pltpu.VMEM((count, columns), jnp.float32),
-            pltpu.VMEM((count, columns), jnp.bfloat16),
             pltpu.VMEM((count, split), jnp.bfloat16),
             pltpu.VMEM((images, heads * STEPS, HD), jnp.float32),
             pltpu.VMEM((images, heads * STEPS, window), jnp.float32),
             pltpu.VMEM((images, heads * STEPS, window), jnp.bfloat16),
             pltpu.VMEM((images, STEPS, full + LANES), queries.dtype),
             pltpu.SemaphoreType.DMA,
-            pltpu.SemaphoreType.DMA((2, PIECES)),
+            pltpu.SemaphoreType.DMA((RUNS,)),
             pltpu.SemaphoreType.DMA((images,)),
         ],
         compiler_params=pltpu.CompilerParams(vmem_limit_bytes=32 << 20),
         name="visual_attention",
-    )(places, queries, ours, *received)
+    )(places, queries, received, ours)
 
 
 def merge(slot_of_row, returned, cached, rows):
-    full = cached.shape[2] - LANES
+    full = cached.shape[1] - LANES
     heads = full // HD
-    runs = 3 if rows % 3 == 0 else 1
-    run = rows // runs
-
-    def kernel(slot_hbm, returned_ref, cached_hbm, out_hbm, slot_ref, cached_s, out_s, slot_sem, sems):
+    count = rows * STEPS
+    block = 2 * STEPS
+    runs = 3 if rows % 6 == 0 else 1
+    run = count // runs
+
+    def kernel(
+        slot_hbm, returned_ref, cached_hbm, out_hbm, slot_ref, cached_s, other_s, out_s, slot_sem, sems
+    ):
         read_slots = pltpu.make_async_copy(slot_hbm, slot_ref, slot_sem)
         read_slots.start()
         loads = []
-        stores = []
         for k in range(runs):
             span = pl.ds(k * run, run)
             load = pltpu.make_async_copy(cached_hbm.at[span], cached_s.at[span], sems.at[0, k])
             load.start()
             loads.append(load)
         read_slots.wait()
+        for r in range(rows):
+            present = slot_ref[r] >= 0
+            other = returned_ref[jnp.maximum(slot_ref[r], 0)].astype(jnp.float32)
+            span = slice(r * STEPS, (r + 1) * STEPS)
+            other_s[span, :full] = jnp.where(present, other[:, :full], 0.0)
+            other_s[span, full:] = jnp.where(present, other[:, full:], FLOOR)
+        stores = []
         for k in range(runs):
             loads[k].wait()
-            for r in range(k * run, (k + 1) * run):
-                present = slot_ref[r] >= 0
-                slot = jnp.maximum(slot_ref[r], 0)
-                terms = returned_ref[slot, :, full:].astype(jnp.float32)
+            for at in range(k * run, (k + 1) * run, block):
+                span = slice(at, at + block)
+                terms = other_s[span, full:]
                 log = (
                     terms[:, :heads] + terms[:, heads : 2 * heads] + terms[:, 2 * heads : 3 * heads]
                 )
-                share = 1.0 / (1.0 + jnp.exp(cached_s[r, :, full : full + heads] - log))
+                share = 1.0 / (1.0 + jnp.exp(cached_s[span, full : full + heads] - log))
                 for h in range(heads):
                     lanes = slice(h * HD, (h + 1) * HD)
-                    own = cached_s[r, :, lanes]
-                    other = returned_ref[slot, :, lanes].astype(jnp.float32)
-                    mixed = own + share[:, h : h + 1] * (other - own)
-                    out_s[r, :, lanes] = jnp.where(present, mixed, own).astype(out_s.dtype)
-            span = pl.ds(k * run, run)
+                    own = cached_s[span, lanes]
+                    mixed = own + share[:, h : h + 1] * (other_s[span, lanes] - own)
+                    mixed = mixed.astype(out_s.dtype).reshape(block // STEPS, STEPS, HD)
+                    out_s[at // STEPS : (at + block) // STEPS, :, lanes] = mixed
+            span = pl.ds(k * run // STEPS, run // STEPS)
             store = pltpu.make_async_copy(out_s.at[span], out_hbm.at[span], sems.at[1, k])
             store.start()
             stores.append(store)
@@ -461,16 +489,13 @@
     anywhere = pl.BlockSpec(memory_space=pl.ANY)
     return pl.pallas_call(
         kernel,
-        in_specs=[
-            anywhere,
-            pl.BlockSpec(memory_space=pltpu.VMEM),
-            anywhere,
-        ],
+        in_specs=[anywhere, pl.BlockSpec(memory_space=pltpu.VMEM), anywhere],
         out_specs=anywhere,
         out_shape=jax.ShapeDtypeStruct((rows, STEPS, full), jnp.bfloat16),
         scratch_shapes=[
             pltpu.SMEM(slot_of_row.shape, jnp.int32),
-            pltpu.VMEM((rows, STEPS, full + LANES), jnp.float32),
+            pltpu.VMEM((count, full + LANES), jnp.float32),
+            pltpu.VMEM((count, full + LANES), jnp.float32),
             pltpu.VMEM((rows, STEPS, full), jnp.bfloat16),
             pltpu.SemaphoreType.DMA,
             pltpu.SemaphoreType.DMA((2, runs)),
@@ -499,9 +524,9 @@
     weight_half = kv_weight[0]
     packed, slot_of_row = pack_queries(image_owner, step_queries, devices, capacity)
     tokens, packed = lax.optimization_barrier((visual_tokens, packed))
-    asked = lax.all_to_all(packed, "dp", split_axis=0, concat_axis=0, tiled=True)
+    asked = exchange(packed, devices)
     for_partner, ours = project(tokens, weight_half)
-    from_partner = [lax.ppermute(piece, "tensor", [(0, 1), (1, 0)]) for piece in for_partner]
+    from_partner = lax.ppermute(for_partner, "tensor", [(0, 1), (1, 0)])
 
     cached = cached_attention(
         step_queries, cache_keys, cache_values, step_keys, step_values, cache_lengths
@@ -519,12 +544,17 @@
     )
     starts = jnp.sum(jnp.where(earlier, own_lengths[None, :], 0), axis=1)
     window_at = jnp.minimum(starts // 16 * 16, visual_tokens.shape[0] - VMAX - 16)
+    order_of_place = jnp.array(exchange_order(devices), jnp.int32)
+    own_place = jnp.sum(
+        jnp.where(own_device[:, None] == order_of_place[None, :], jnp.arange(devices)[None, :], 0),
+        axis=1,
+    )
     places = jnp.concatenate(
-        [own_device * capacity + own_rank, window_at, starts - window_at, own_lengths]
+        [own_place * capacity + own_rank, window_at, starts - window_at, own_lengths]
     )
 
     answers = visual_attention(places, asked, ours, from_partner)
-    returned = lax.all_to_all(answers, "dp", split_axis=0, concat_axis=0, tiled=True)
+    returned = exchange(answers, devices)
     return merge(slot_of_row, returned, cached, rows_local)
 
 

time: 45.3 us -> 41.5 us (0.916)
  waiting for transfers between devices: 8.17 us -> 4.35 us
    all_to_all x2, waiting for transfers between devices: 7.03 us -> 2.73 us  [exchange(): lax.all_to_all(slots, 'dp', split_axis=0, concat_axis=0, tiled=True, axis...]
    all_to_all x2, starting transfers between devices: 12.6 us -> 13.5 us  [exchange(): lax.all_to_all(slots, 'dp', split_axis=0, concat_axis=0, tiled=True, axis...]
    pallas_call x1, Pallas kernels: 3.07 us -> 2.5 us  [merge(): pl.pallas_call(kernel, in_specs=[anywhere, pl.BlockSpec(memory_space=pltp...]
    ppermute x2 -> x1, starting transfers between devices: 0.57 us -> 0.07 us  [shards(): from_partner = lax.ppermute(for_partner, 'tensor', [(0, 1), (1, 0)])]
    ppermute x2 -> x1, waiting for transfers between devices: 1.15 us -> 1.62 us  [shards(): from_partner = lax.ppermute(for_partner, 'tensor', [(0, 1), (1, 0)])]
  transfers between devices with their start and end apart: 4 -> 3, of which waited for: 4 -> 2; matrix products, arithmetic and copies ran while one was open for 1% -> 1% of each run, Pallas kernels for 33% -> 36%
where the time goes in v4:
time: 41.5 us; the launch traced here: 41.1 us
  Pallas kernels  22.5 us (54%)
  starting transfers between devices  13.6 us (33%)
  waiting for transfers between devices  4.35 us (10%)
  other arithmetic  0.57 us (1%)
    all_to_all x2, starting transfers between devices, exchange(): lax.all_to_all(slots, 'dp', split_axis=0, concat_axis=0, tiled=True, axis...  13.5 us
    pallas_call x1, Pallas kernels, project(): pl.pallas_call(kernel, in_specs=[hbm, hbm], out_specs=[pl.BlockSpec(memor...  8.66 us
    pallas_call x1, Pallas kernels, cached_attention(): pl.pallas_call(kernel, grid_spec=pltpu.PrefetchScalarGridSpec(num_scalar_...  6.3 us
    pallas_call x1, Pallas kernels, visual_attention(): pl.pallas_call(kernel, in_specs=[anywhere, vmem, vmem, anywhere], out_spe...  2.87 us
    all_to_all x2, waiting for transfers between devices, exchange(): lax.all_to_all(slots, 'dp', split_axis=0, concat_axis=0, tiled=True, axis...  2.73 us
    pallas_call x1, Pallas kernels, merge(): pl.pallas_call(kernel, in_specs=[anywhere, pl.BlockSpec(memory_space=pltp...  2.5 us
    pallas_call x1, Pallas kernels, pack_queries(): pl.pallas_call(kernel, in_specs=[pl.BlockSpec(memory_space=pl.ANY), pl.Bl...  2.13 us
    ppermute x1, waiting for transfers between devices, shards(): from_partner = lax.ppermute(for_partner, 'tensor', [(0, 1), (1, 0)])  1.62 us
  transfers between devices with their start and end apart: 3, of which 2 were waited for; matrix products, arithmetic and copies ran while one was open for 1% of the time, Pallas kernels for 36%

profile of v4, /device:TPU:0, one launch (start us, length us, event | category | flops | bytes accessed | tf_op | source)
XLA Modules:
  0.0 41.1 jit_solution(17080227867678098673)
XLA Ops:
  0.0 0.0 copy-start
  0.0 0.0 copy-start.4
  0.0 0.0 copy-start.3
  0.0 2.1 %pack_queries.1 = (bf16[24,4,2048]{2,1,0:T(4,128)(2,1)}, s32[128]{0:T(128)}) custom-call(s32[96]{0:T(128)} %owner_hbm.1, bf16[24,4,2048]{2,1,0:T(4,128)(2,1)} %q_ref.1), custom_call_target="tpu_custom_call" | custom-call | tf_op jit(solution)/shard_map/pack_queries/pallas_call | solution.py:96
  2.1 8.4 %all-to-all-start = ((bf16[24,4,2048]{2,1,0:T(4,128)(2,1)}), bf16[24,4,2048]{2,1,0:T(4,128)(2,1)S(1)}, u32[]{:S(2)}, u32[]{:S(2)}) async-start(bf16[24,4,2048]{2,1,0:T(4,128)(2,1)} %get-tuple-element.13), calls=%async_computation | async-start | bytes 786432 | tf_op jit(solution)/shard_map/all_to_all | solution.py:25
  10.6 8.7 %project.1 = (bf16[480,640]{1,0:T(8,128)(2,1)}, f32[14745,640]{1,0:T(8,128)}) custom-call(bf16[480,4096]{1,0:T(8,128)(2,1)} %token_hbm, bf16[4096,2,512]{2,1,0:T(2,128)(2,1)} %bitcast.3), custom_call_target="tpu_custom_call" | custom-call | flops 1048576 | bytes 65536 | tf_op jit(solution)/shard_map/project/pallas_call | solution.py:192
  19.2 0.1 collective-permute-start
  19.3 0.0 copy-done.3
  19.3 0.1 and_select_fusion.1
  19.4 0.2 convert_reduce_fusion
  19.6 0.0 copy-done.4
  19.6 0.1 select_reduce_fusion.1
  19.7 0.0 copy-done
  19.7 0.1 select_reduce_fusion
  19.8 0.1 pad_add_fusion.place_hbm
  19.9 1.6 %collective-permute-done.received_ref = bf16[480,640]{1,0:T(8,128)(2,1)S(1)} collective-permute-done((bf16[480,640]{1,0:T(8,128)(2,1)}, bf16[480,640]{1,0:T(8,128)(2,1)S(1)}, u32[]{:S(2)}, u32[]{:S(2)}) %collective-permute-start) | collective-permute-done | bytes 614432 | tf_op jit(solution)/shard_map/ppermute | solution.py:529
  21.5 0.0 all-to-all-done.q_ref
  21.5 2.9 %visual_attention.1 = bf16[24,4,2176]{2,1,0:T(4,128)(2,1)} custom-call(s32[48]{0:T(128)S(1)} %pad_add_fusion.place_hbm, bf16[24,4,2048]{2,1,0:T(4,128)(2,1)S(1)} %all-to-all-done.q_ref, bf16[480,640]{1,0:T(8,128)(2,1)S(1)} %collective-permute-done.received_ref, f32[14745,640]{1,0:T(8,128)} %get-tuple-element.16.ours_hbm), custom_call_target="tpu_custom_call" | custom-call | tf_op jit(solution)/shard_map/visual_attention/pallas_call | solution.py:413
  24.4 5.1 %all-to-all-start.1 = ((bf16[24,4,2176]{2,1,0:T(4,128)(2,1)}), bf16[24,4,2176]{2,1,0:T(4,128)(2,1)S(1)}, u32[]{:S(2)}, u32[]{:S(2)}) async-start(bf16[24,4,2176]{2,1,0:T(4,128)(2,1)} %visual_attention.1), calls=%async_computation.1 | async-start | bytes 835584 | tf_op jit(solution)/shard_map/all_to_all | solution.py:25
  29.5 0.0 copy-start.2
  29.5 6.3 %cached_attention.1.cached_hbm = f32[4336,2176]{1,0:T(8,128)} custom-call(s32[24]{0:T(128)} %length_ref.1, bf16[24,4,2048]{2,1,0:T(4,128)(2,1)} %q_ref.1, bf16[24,128,256]{2,1,0:T(8,128)(2,1)} %k_ref.1, bf16[24,128,256]{2,1,0:T(8,128)(2,1)} %v_ref.1, bf16[24,4,256]{2,1,0:T(4,128)(2,1)} %sk_ref.1, bf16[24,4,256]{2,1,0:T(4,128)(2,1)} %sv_ref.1), custom_call_target="tpu_custom_call" | custom-call | flops 1048576 | bytes 65536 | tf_op jit(solution)/shard_map/cached_attention/pallas_call | solution.py:278
  35.8 2.7 %all-to-all-done.1.returned_ref = bf16[24,4,2176]{2,1,0:T(4,128)(2,1)S(1)} async-done(((bf16[24,4,2176]{2,1,0:T(4,128)(2,1)}), bf16[24,4,2176]{2,1,0:T(4,128)(2,1)S(1)}, u32[]{:S(2)}, u32[]{:S(2)}) %all-to-all-start.1) | async-done | bytes 417824 | tf_op jit(solution)/shard_map/all_to_all | solution.py:25
  38.6 0.0 copy-done.2
  38.6 0.0 copy-start.1
  38.6 2.5 %merge.1 = bf16[24,4,2048]{2,1,0:T(4,128)(2,1)} custom-call(s32[128]{0:T(128)S(1)} %copy-done.2, bf16[24,4,2176]{2,1,0:T(4,128)(2,1)S(1)} %all-to-all-done.1.returned_ref, f32[4336,2176]{1,0:T(8,128)} %cached_attention.1.cached_hbm), custom_call_target="tpu_custom_call" | custom-call | tf_op jit(solution)/shard_map/merge/pallas_call | solution.py:490
  41.1 0.0 copy-done.1
  (3 shorter events, 0.0 us)
Async XLA Ops:
  0.0 19.7 %copy-start = (s32[8,12]{1,0:T(8,128)S(1)}, s32[8,12]{1,0:T(8,128)}, u32[]{:S(2)}) copy-start(s32[8,12]{1,0:T(8,128)} %param.13) | copy-start | bytes 1156
  0.0 19.6 %copy-start.4 = (s32[8]{0:T(128)S(1)}, s32[8]{0:T(128)}, u32[]{:S(2)}) copy-start(s32[8]{0:T(128)} %constant.46.clone) | copy-start | bytes 100
  0.0 19.3 %copy-start.3 = (s32[96]{0:T(128)S(1)}, s32[96]{0:T(128)}, u32[]{:S(2)}) copy-start(s32[96]{0:T(128)} %owner_hbm.1) | copy-start | bytes 1156
  2.1 19.4 %all-to-all-start = ((bf16[24,4,2048]{2,1,0:T(4,128)(2,1)}), bf16[24,4,2048]{2,1,0:T(4,128)(2,1)S(1)}, u32[]{:S(2)}, u32[]{:S(2)}) async-start(bf16[24,4,2048]{2,1,0:T(4,128)(2,1)} %get-tuple-element.13), calls=%async_computation | async-start | bytes 786432 | tf_op jit(solution)/shard_map/all_to_all | solution.py:25
  19.2 2.3 %collective-permute-start = (bf16[480,640]{1,0:T(8,128)(2,1)}, bf16[480,640]{1,0:T(8,128)(2,1)S(1)}, u32[]{:S(2)}, u32[]{:S(2)}) collective-permute-start(bf16[480,640]{1,0:T(8,128)(2,1)} %get-tuple-element.15), channel_id=1, source_target_pairs={{0,1},{1,0},{2,3},{3,2},{4,5},{5,4},{6,7},{7,6},{8,9},{9,8},{10,11... | collective-permute-start | bytes 1843208 | tf_op jit(solution)/shard_map/ppermute | solution.py:529
  24.4 14.1 %all-to-all-start.1 = ((bf16[24,4,2176]{2,1,0:T(4,128)(2,1)}), bf16[24,4,2176]{2,1,0:T(4,128)(2,1)S(1)}, u32[]{:S(2)}, u32[]{:S(2)}) async-start(bf16[24,4,2176]{2,1,0:T(4,128)(2,1)} %visual_attention.1), calls=%async_computation.1 | async-start | bytes 835584 | tf_op jit(solution)/shard_map/all_to_all | solution.py:25
  29.5 9.0 %copy-start.2 = (s32[128]{0:T(128)S(1)}, s32[128]{0:T(128)}, u32[]{:S(2)}) copy-start(s32[128]{0:T(128)} %get-tuple-element.11.slot_hbm) | copy-start | bytes 1540
  38.6 2.5 %copy-start.1 = (s32[8,12]{1,0:T(8,128)S(1)}, s32[8,12]{1,0:T(8,128)}, u32[]{:S(2)}) copy-start(s32[8,12]{1,0:T(8,128)} %param.13) | copy-start | bytes 1156

commit v5 on v4

--- a/solution.py
+++ b/solution.py
@@ -12,8 +12,8 @@
 EPSILON = 1e-06
 LANES = 128
 FLOOR = -1e30
-RUNS = 4
-ORDERS = {8: (5, 6, 4, 3, 1, 7, 2, 0)}
+RUNS = 2
+ORDERS = {8: (5, 7, 4, 1, 3, 6, 2, 0)}
 FAR_BYTES = 36 << 20
 
 

time: 41.5 us -> 40.8 us (0.983)
  waiting for transfers between devices: 4.35 us -> 3.69 us
    all_to_all x2, waiting for transfers between devices: 2.73 us -> 2.07 us  [exchange(): lax.all_to_all(slots, 'dp', split_axis=0, concat_axis=0, tiled=True, axis...]
  transfers between devices with their start and end apart: 3 -> 3, of which waited for: 2 -> 2; matrix products, arithmetic and copies ran while one was open for 1% -> 1% of each run, Pallas kernels for 36% -> 37%
where the time goes in v5:
time: 40.8 us; the launch traced here: 40.3 us
  Pallas kernels  22.4 us (55%)
  starting transfers between devices  13.6 us (33%)
  waiting for transfers between devices  3.69 us (9%)
  other arithmetic  0.57 us (1%)
    all_to_all x2, starting transfers between devices, exchange(): lax.all_to_all(slots, 'dp', split_axis=0, concat_axis=0, tiled=True, axis...  13.5 us
    pallas_call x1, Pallas kernels, project(): pl.pallas_call(kernel, in_specs=[hbm, hbm], out_specs=[pl.BlockSpec(memor...  8.66 us
    pallas_call x1, Pallas kernels, cached_attention(): pl.pallas_call(kernel, grid_spec=pltpu.PrefetchScalarGridSpec(num_scalar_...  6.3 us
    pallas_call x1, Pallas kernels, visual_attention(): pl.pallas_call(kernel, in_specs=[anywhere, vmem, vmem, anywhere], out_spe...  2.81 us
    pallas_call x1, Pallas kernels, merge(): pl.pallas_call(kernel, in_specs=[anywhere, pl.BlockSpec(memory_space=pltp...  2.5 us
    pallas_call x1, Pallas kernels, pack_queries(): pl.pallas_call(kernel, in_specs=[pl.BlockSpec(memory_space=pl.ANY), pl.Bl...  2.13 us
    all_to_all x2, waiting for transfers between devices, exchange(): lax.all_to_all(slots, 'dp', split_axis=0, concat_axis=0, tiled=True, axis...  2.07 us
    ppermute x1, waiting for transfers between devices, shards(): from_partner = lax.ppermute(for_partner, 'tensor', [(0, 1), (1, 0)])  1.62 us
  transfers between devices with their start and end apart: 3, of which 2 were waited for; matrix products, arithmetic and copies ran while one was open for 1% of the time, Pallas kernels for 37%

profile of v5, /device:TPU:0, one launch (start us, length us, event | category | flops | bytes accessed | tf_op | source)
XLA Modules:
  0.0 40.3 jit_solution(17366981342672547389)
XLA Ops:
  0.0 0.0 copy-start
  0.0 0.0 copy-start.4
  0.0 0.0 copy-start.3
  0.0 2.1 %pack_queries.1 = (bf16[24,4,2048]{2,1,0:T(4,128)(2,1)}, s32[128]{0:T(128)}) custom-call(s32[96]{0:T(128)} %owner_hbm.1, bf16[24,4,2048]{2,1,0:T(4,128)(2,1)} %q_ref.1), custom_call_target="tpu_custom_call" | custom-call | tf_op jit(solution)/shard_map/pack_queries/pallas_call | solution.py:96
  2.1 8.4 %all-to-all-start = ((bf16[24,4,2048]{2,1,0:T(4,128)(2,1)}), bf16[24,4,2048]{2,1,0:T(4,128)(2,1)S(1)}, u32[]{:S(2)}, u32[]{:S(2)}) async-start(bf16[24,4,2048]{2,1,0:T(4,128)(2,1)} %get-tuple-element.13), calls=%async_computation | async-start | bytes 786432 | tf_op jit(solution)/shard_map/all_to_all | solution.py:25
  10.6 8.7 %project.1 = (bf16[480,640]{1,0:T(8,128)(2,1)}, f32[14745,640]{1,0:T(8,128)}) custom-call(bf16[480,4096]{1,0:T(8,128)(2,1)} %token_hbm, bf16[4096,2,512]{2,1,0:T(2,128)(2,1)} %bitcast.3), custom_call_target="tpu_custom_call" | custom-call | flops 1048576 | bytes 65536 | tf_op jit(solution)/shard_map/project/pallas_call | solution.py:192
  19.2 0.1 collective-permute-start
  19.3 0.0 copy-done.3
  19.3 0.1 and_select_fusion.1
  19.4 0.2 convert_reduce_fusion
  19.6 0.0 copy-done.4
  19.6 0.1 select_reduce_fusion.1
  19.7 0.0 copy-done
  19.7 0.1 select_reduce_fusion
  19.8 0.1 pad_add_fusion.place_hbm
  19.9 1.6 %collective-permute-done.received_ref = bf16[480,640]{1,0:T(8,128)(2,1)S(1)} collective-permute-done((bf16[480,640]{1,0:T(8,128)(2,1)}, bf16[480,640]{1,0:T(8,128)(2,1)S(1)}, u32[]{:S(2)}, u32[]{:S(2)}) %collective-permute-start) | collective-permute-done | bytes 614432 | tf_op jit(solution)/shard_map/ppermute | solution.py:529
  21.5 0.0 all-to-all-done.q_ref
  21.5 2.8 %visual_attention.1 = bf16[24,4,2176]{2,1,0:T(4,128)(2,1)} custom-call(s32[48]{0:T(128)S(1)} %pad_add_fusion.place_hbm, bf16[24,4,2048]{2,1,0:T(4,128)(2,1)S(1)} %all-to-all-done.q_ref, bf16[480,640]{1,0:T(8,128)(2,1)S(1)} %collective-permute-done.received_ref, f32[14745,640]{1,0:T(8,128)} %get-tuple-element.16.ours_hbm), custom_call_target="tpu_custom_call" | custom-call | tf_op jit(solution)/shard_map/visual_attention/pallas_call | solution.py:413
  24.4 5.1 %all-to-all-start.1 = ((bf16[24,4,2176]{2,1,0:T(4,128)(2,1)}), bf16[24,4,2176]{2,1,0:T(4,128)(2,1)S(1)}, u32[]{:S(2)}, u32[]{:S(2)}) async-start(bf16[24,4,2176]{2,1,0:T(4,128)(2,1)} %visual_attention.1), calls=%async_computation.1 | async-start | bytes 835584 | tf_op jit(solution)/shard_map/all_to_all | solution.py:25
  29.5 0.0 copy-start.2
  29.5 6.3 %cached_attention.1.cached_hbm = f32[4336,2176]{1,0:T(8,128)} custom-call(s32[24]{0:T(128)} %length_ref.1, bf16[24,4,2048]{2,1,0:T(4,128)(2,1)} %q_ref.1, bf16[24,128,256]{2,1,0:T(8,128)(2,1)} %k_ref.1, bf16[24,128,256]{2,1,0:T(8,128)(2,1)} %v_ref.1, bf16[24,4,256]{2,1,0:T(4,128)(2,1)} %sk_ref.1, bf16[24,4,256]{2,1,0:T(4,128)(2,1)} %sv_ref.1), custom_call_target="tpu_custom_call" | custom-call | flops 1048576 | bytes 65536 | tf_op jit(solution)/shard_map/cached_attention/pallas_call | solution.py:278
  35.8 2.1 %all-to-all-done.1.returned_ref = bf16[24,4,2176]{2,1,0:T(4,128)(2,1)S(1)} async-done(((bf16[24,4,2176]{2,1,0:T(4,128)(2,1)}), bf16[24,4,2176]{2,1,0:T(4,128)(2,1)S(1)}, u32[]{:S(2)}, u32[]{:S(2)}) %all-to-all-start.1) | async-done | bytes 417824 | tf_op jit(solution)/shard_map/all_to_all | solution.py:25
  37.8 0.0 copy-done.2
  37.8 0.0 copy-start.1
  37.8 2.5 %merge.1 = bf16[24,4,2048]{2,1,0:T(4,128)(2,1)} custom-call(s32[128]{0:T(128)S(1)} %copy-done.2, bf16[24,4,2176]{2,1,0:T(4,128)(2,1)S(1)} %all-to-all-done.1.returned_ref, f32[4336,2176]{1,0:T(8,128)} %cached_attention.1.cached_hbm), custom_call_target="tpu_custom_call" | custom-call | tf_op jit(solution)/shard_map/merge/pallas_call | solution.py:490
  40.3 0.0 copy-done.1
  (3 shorter events, 0.0 us)
Async XLA Ops:
  0.0 19.7 %copy-start = (s32[8,12]{1,0:T(8,128)S(1)}, s32[8,12]{1,0:T(8,128)}, u32[]{:S(2)}) copy-start(s32[8,12]{1,0:T(8,128)} %param.13) | copy-start | bytes 1156
  0.0 19.6 %copy-start.4 = (s32[8]{0:T(128)S(1)}, s32[8]{0:T(128)}, u32[]{:S(2)}) copy-start(s32[8]{0:T(128)} %constant.46.clone) | copy-start | bytes 100
  0.0 19.3 %copy-start.3 = (s32[96]{0:T(128)S(1)}, s32[96]{0:T(128)}, u32[]{:S(2)}) copy-start(s32[96]{0:T(128)} %owner_hbm.1) | copy-start | bytes 1156
  2.1 19.4 %all-to-all-start = ((bf16[24,4,2048]{2,1,0:T(4,128)(2,1)}), bf16[24,4,2048]{2,1,0:T(4,128)(2,1)S(1)}, u32[]{:S(2)}, u32[]{:S(2)}) async-start(bf16[24,4,2048]{2,1,0:T(4,128)(2,1)} %get-tuple-element.13), calls=%async_computation | async-start | bytes 786432 | tf_op jit(solution)/shard_map/all_to_all | solution.py:25
  19.2 2.3 %collective-permute-start = (bf16[480,640]{1,0:T(8,128)(2,1)}, bf16[480,640]{1,0:T(8,128)(2,1)S(1)}, u32[]{:S(2)}, u32[]{:S(2)}) collective-permute-start(bf16[480,640]{1,0:T(8,128)(2,1)} %get-tuple-element.15), channel_id=1, source_target_pairs={{0,1},{1,0},{2,3},{3,2},{4,5},{5,4},{6,7},{7,6},{8,9},{9,8},{10,11... | collective-permute-start | bytes 1843208 | tf_op jit(solution)/shard_map/ppermute | solution.py:529
  24.4 13.5 %all-to-all-start.1 = ((bf16[24,4,2176]{2,1,0:T(4,128)(2,1)}), bf16[24,4,2176]{2,1,0:T(4,128)(2,1)S(1)}, u32[]{:S(2)}, u32[]{:S(2)}) async-start(bf16[24,4,2176]{2,1,0:T(4,128)(2,1)} %visual_attention.1), calls=%async_computation.1 | async-start | bytes 835584 | tf_op jit(solution)/shard_map/all_to_all | solution.py:25
  29.5 8.4 %copy-start.2 = (s32[128]{0:T(128)S(1)}, s32[128]{0:T(128)}, u32[]{:S(2)}) copy-start(s32[128]{0:T(128)} %get-tuple-element.11.slot_hbm) | copy-start | bytes 1540
  37.8 2.5 %copy-start.1 = (s32[8,12]{1,0:T(8,128)S(1)}, s32[8,12]{1,0:T(8,128)}, u32[]{:S(2)}) copy-start(s32[8,12]{1,0:T(8,128)} %param.13) | copy-start | bytes 1156

commit v6 on v5

--- a/solution.py
+++ b/solution.py
@@ -123,7 +123,7 @@
     ahead = 3
 
     def kernel(
-        token_hbm, weight_hbm, theirs_ref, ours_hbm, ours_s, token_s, weight_s, sems, out_sem
+        token_hbm, weight_hbm, theirs_ref, ours_hbm, total_s, ours_s, token_s, weight_s, sems, out_sem
     ):
         mine = lax.axis_index("tensor")
 
@@ -171,17 +171,18 @@
             x = token_s[:, span]
             part = product(x, weight_s[0, span])
             if c == 0:
-                ours_s[:, : 2 * width] = part
+                total_s[...] = part
             else:
-                ours_s[:, : 2 * width] += part
+                total_s[...] += part
             for lane in range(0, sizes[c], LANES):
                 wide = x[:, lane : lane + LANES].astype(jnp.float32)
                 squares += wide * wide
         squares = jnp.broadcast_to(jnp.sum(squares, axis=1, keepdims=True), (count, LANES))
-        ours_s[:, 2 * width :] = squares
+        terms = three_terms(squares, lax.broadcasted_iota(jnp.int32, (count, LANES), 1), 1)
+        ours_s[:, : 2 * width] = total_s[...].astype(jnp.bfloat16)
+        ours_s[:, 2 * width :] = terms
         store = pltpu.make_async_copy(ours_s, ours_hbm.at[pl.ds(0, count)], out_sem)
         store.start()
-        terms = three_terms(squares, lax.broadcasted_iota(jnp.int32, (count, LANES), 1), 1)
         for load in loads[chunks]:
             load.wait()
         theirs_ref[:, : 2 * width] = product(token_s[...], weight_s[1]).astype(jnp.bfloat16)
@@ -195,10 +196,11 @@
         out_specs=[pl.BlockSpec(memory_space=pltpu.VMEM), pl.BlockSpec(memory_space=pl.ANY)],
         out_shape=[
             jax.ShapeDtypeStruct((count, columns), jnp.bfloat16),
-            jax.ShapeDtypeStruct((FAR_BYTES // (4 * columns), columns), jnp.float32),
+            jax.ShapeDtypeStruct((FAR_BYTES // (2 * columns), columns), jnp.bfloat16),
         ],
         scratch_shapes=[
-            pltpu.VMEM((count, columns), jnp.float32),
+            pltpu.VMEM((count, 2 * width), jnp.float32),
+            pltpu.VMEM((count, columns), jnp.bfloat16),
             pltpu.VMEM(tokens.shape, tokens.dtype),
             pltpu.VMEM((2, depth, 2, width), weight.dtype),
             pltpu.SemaphoreType.DMA((3, chunks)),
@@ -355,14 +357,16 @@
         for k in range(RUNS):
             loads[k].wait()
             rows = slice(k * run, (k + 1) * run)
-            squares = jnp.sum(
-                received_ref[rows, split:].astype(jnp.float32), axis=1, keepdims=True
-            )
-            factor = lax.rsqrt((ours_s[rows, split:] + squares) / D + EPSILON)
+            squares = ours_s[rows, split:].astype(jnp.float32) + received_ref[
+                rows, split:
+            ].astype(jnp.float32)
+            factor = lax.rsqrt(jnp.sum(squares, axis=1, keepdims=True) / D + EPSILON)
             for at in range(0, split, LANES):
                 lanes = slice(at, at + LANES)
-                total = (ours_s[rows, lanes] + received_ref[rows, lanes].astype(jnp.float32)) * factor
-                pair_ref[rows, lanes] = total.astype(pair_ref.dtype)
+                total = ours_s[rows, lanes].astype(jnp.float32) + received_ref[rows, lanes].astype(
+                    jnp.float32
+                )
+                pair_ref[rows, lanes] = (total * factor).astype(pair_ref.dtype)
         for i in range(images):
             rows = pl.ds(pl.multiple_of(place_ref[1 * images + i], 16), window)
             q = q_s[i].astype(jnp.bfloat16)
@@ -422,7 +426,7 @@
         out_shape=jax.ShapeDtypeStruct((slots, STEPS, full + LANES), queries.dtype),
         scratch_shapes=[
             pltpu.SMEM(places.shape, jnp.int32),
-            pltpu.VMEM((count, columns), jnp.float32),
+            pltpu.VMEM((count, columns), jnp.bfloat16),
             pltpu.VMEM((count, split), jnp.bfloat16),
             pltpu.VMEM((images, heads * STEPS, HD), jnp.float32),
             pltpu.VMEM((images, heads * STEPS, window), jnp.float32),

time: 40.8 us -> 40.6 us (level)
  no operation moved by 1% of the time
where the time goes in v6:
time: 40.6 us; the launch traced here: 40.2 us
  Pallas kernels  22.3 us (55%)
  starting transfers between devices  13.6 us (33%)
  waiting for transfers between devices  3.69 us (9%)
  other arithmetic  0.57 us (1%)
    all_to_all x2, starting transfers between devices, exchange(): lax.all_to_all(slots, 'dp', split_axis=0, concat_axis=0, tiled=True, axis...  13.5 us
    pallas_call x1, Pallas kernels, project(): pl.pallas_call(kernel, in_specs=[hbm, hbm], out_specs=[pl.BlockSpec(memor...  8.67 us
    pallas_call x1, Pallas kernels, cached_attention(): pl.pallas_call(kernel, grid_spec=pltpu.PrefetchScalarGridSpec(num_scalar_...  6.3 us
    pallas_call x1, Pallas kernels, visual_attention(): pl.pallas_call(kernel, in_specs=[anywhere, vmem, vmem, anywhere], out_spe...  2.68 us
    pallas_call x1, Pallas kernels, merge(): pl.pallas_call(kernel, in_specs=[anywhere, pl.BlockSpec(memory_space=pltp...  2.5 us
    pallas_call x1, Pallas kernels, pack_queries(): pl.pallas_call(kernel, in_specs=[pl.BlockSpec(memory_space=pl.ANY), pl.Bl...  2.13 us
    all_to_all x2, waiting for transfers between devices, exchange(): lax.all_to_all(slots, 'dp', split_axis=0, concat_axis=0, tiled=True, axis...  2.07 us
    ppermute x1, waiting for transfers between devices, shards(): from_partner = lax.ppermute(for_partner, 'tensor', [(0, 1), (1, 0)])  1.62 us
  transfers between devices with their start and end apart: 3, of which 2 were waited for; matrix products, arithmetic and copies ran while one was open for 1% of the time, Pallas kernels for 37%

profile of v6, /device:TPU:0, one launch (start us, length us, event | category | flops | bytes accessed | tf_op | source)
XLA Modules:
  0.0 40.2 jit_solution(7339874708803058160)
XLA Ops:
  0.0 0.0 copy-start
  0.0 0.0 copy-start.4
  0.0 0.0 copy-start.3
  0.0 2.1 %pack_queries.1 = (bf16[24,4,2048]{2,1,0:T(4,128)(2,1)}, s32[128]{0:T(128)}) custom-call(s32[96]{0:T(128)} %owner_hbm.1, bf16[24,4,2048]{2,1,0:T(4,128)(2,1)} %q_ref.1), custom_call_target="tpu_custom_call" | custom-call | tf_op jit(solution)/shard_map/pack_queries/pallas_call | solution.py:96
  2.1 8.4 %all-to-all-start = ((bf16[24,4,2048]{2,1,0:T(4,128)(2,1)}), bf16[24,4,2048]{2,1,0:T(4,128)(2,1)S(1)}, u32[]{:S(2)}, u32[]{:S(2)}) async-start(bf16[24,4,2048]{2,1,0:T(4,128)(2,1)} %get-tuple-element.13), calls=%async_computation | async-start | bytes 786432 | tf_op jit(solution)/shard_map/all_to_all | solution.py:25
  10.6 8.7 %project.1 = (bf16[480,640]{1,0:T(8,128)(2,1)}, bf16[29491,640]{1,0:T(8,128)(2,1)}) custom-call(bf16[480,4096]{1,0:T(8,128)(2,1)} %token_hbm, bf16[4096,2,512]{2,1,0:T(2,128)(2,1)} %bitcast.3), custom_call_target="tpu_custom_call" | custom-call | flops 1048576 | bytes 65536 | tf_op jit(solution)/shard_map/project/pallas_call | solution.py:193
  19.2 0.1 collective-permute-start
  19.3 0.0 copy-done.3
  19.3 0.1 and_select_fusion.1
  19.4 0.2 convert_reduce_fusion
  19.6 0.0 copy-done.4
  19.6 0.1 select_reduce_fusion.1
  19.7 0.0 copy-done
  19.7 0.1 select_reduce_fusion
  19.8 0.1 pad_add_fusion.place_hbm
  19.9 1.6 %collective-permute-done.received_ref = bf16[480,640]{1,0:T(8,128)(2,1)S(1)} collective-permute-done((bf16[480,640]{1,0:T(8,128)(2,1)}, bf16[480,640]{1,0:T(8,128)(2,1)S(1)}, u32[]{:S(2)}, u32[]{:S(2)}) %collective-permute-start) | collective-permute-done | bytes 614432 | tf_op jit(solution)/shard_map/ppermute | solution.py:533
  21.5 0.0 all-to-all-done.q_ref
  21.5 2.7 %visual_attention.1 = bf16[24,4,2176]{2,1,0:T(4,128)(2,1)} custom-call(s32[48]{0:T(128)S(1)} %pad_add_fusion.place_hbm, bf16[24,4,2048]{2,1,0:T(4,128)(2,1)S(1)} %all-to-all-done.q_ref, bf16[480,640]{1,0:T(8,128)(2,1)S(1)} %collective-permute-done.received_ref, bf16[29491,640]{1,0:T(8,128)(2,1)} %get-tuple-element.16.ours_hbm), custom_call_target="tpu_custom_call" | custom-call | tf_op jit(solution)/shard_map/visual_attention/pallas_call | solution.py:417
  24.2 5.1 %all-to-all-start.1 = ((bf16[24,4,2176]{2,1,0:T(4,128)(2,1)}), bf16[24,4,2176]{2,1,0:T(4,128)(2,1)S(1)}, u32[]{:S(2)}, u32[]{:S(2)}) async-start(bf16[24,4,2176]{2,1,0:T(4,128)(2,1)} %visual_attention.1), calls=%async_computation.1 | async-start | bytes 835584 | tf_op jit(solution)/shard_map/all_to_all | solution.py:25
  29.3 0.0 copy-start.2
  29.3 6.3 %cached_attention.1.cached_hbm = f32[4336,2176]{1,0:T(8,128)} custom-call(s32[24]{0:T(128)} %length_ref.1, bf16[24,4,2048]{2,1,0:T(4,128)(2,1)} %q_ref.1, bf16[24,128,256]{2,1,0:T(8,128)(2,1)} %k_ref.1, bf16[24,128,256]{2,1,0:T(8,128)(2,1)} %v_ref.1, bf16[24,4,256]{2,1,0:T(4,128)(2,1)} %sk_ref.1, bf16[24,4,256]{2,1,0:T(4,128)(2,1)} %sv_ref.1), custom_call_target="tpu_custom_call" | custom-call | flops 1048576 | bytes 65536 | tf_op jit(solution)/shard_map/cached_attention/pallas_call | solution.py:280
  35.6 2.1 %all-to-all-done.1.returned_ref = bf16[24,4,2176]{2,1,0:T(4,128)(2,1)S(1)} async-done(((bf16[24,4,2176]{2,1,0:T(4,128)(2,1)}), bf16[24,4,2176]{2,1,0:T(4,128)(2,1)S(1)}, u32[]{:S(2)}, u32[]{:S(2)}) %all-to-all-start.1) | async-done | bytes 417824 | tf_op jit(solution)/shard_map/all_to_all | solution.py:25
  37.7 0.0 copy-done.2
  37.7 0.0 copy-start.1
  37.7 2.5 %merge.1 = bf16[24,4,2048]{2,1,0:T(4,128)(2,1)} custom-call(s32[128]{0:T(128)S(1)} %copy-done.2, bf16[24,4,2176]{2,1,0:T(4,128)(2,1)S(1)} %all-to-all-done.1.returned_ref, f32[4336,2176]{1,0:T(8,128)} %cached_attention.1.cached_hbm), custom_call_target="tpu_custom_call" | custom-call | tf_op jit(solution)/shard_map/merge/pallas_call | solution.py:494
  40.2 0.0 copy-done.1
  (3 shorter events, 0.0 us)
Async XLA Ops:
  0.0 19.7 %copy-start = (s32[8,12]{1,0:T(8,128)S(1)}, s32[8,12]{1,0:T(8,128)}, u32[]{:S(2)}) copy-start(s32[8,12]{1,0:T(8,128)} %param.13) | copy-start | bytes 1156
  0.0 19.6 %copy-start.4 = (s32[8]{0:T(128)S(1)}, s32[8]{0:T(128)}, u32[]{:S(2)}) copy-start(s32[8]{0:T(128)} %constant.46.clone) | copy-start | bytes 100
  0.0 19.3 %copy-start.3 = (s32[96]{0:T(128)S(1)}, s32[96]{0:T(128)}, u32[]{:S(2)}) copy-start(s32[96]{0:T(128)} %owner_hbm.1) | copy-start | bytes 1156
  2.1 19.4 %all-to-all-start = ((bf16[24,4,2048]{2,1,0:T(4,128)(2,1)}), bf16[24,4,2048]{2,1,0:T(4,128)(2,1)S(1)}, u32[]{:S(2)}, u32[]{:S(2)}) async-start(bf16[24,4,2048]{2,1,0:T(4,128)(2,1)} %get-tuple-element.13), calls=%async_computation | async-start | bytes 786432 | tf_op jit(solution)/shard_map/all_to_all | solution.py:25
  19.2 2.3 %collective-permute-start = (bf16[480,640]{1,0:T(8,128)(2,1)}, bf16[480,640]{1,0:T(8,128)(2,1)S(1)}, u32[]{:S(2)}, u32[]{:S(2)}) collective-permute-start(bf16[480,640]{1,0:T(8,128)(2,1)} %get-tuple-element.15), channel_id=1, source_target_pairs={{0,1},{1,0},{2,3},{3,2},{4,5},{5,4},{6,7},{7,6},{8,9},{9,8},{10,11... | collective-permute-start | bytes 1843208 | tf_op jit(solution)/shard_map/ppermute | solution.py:533
  24.2 13.5 %all-to-all-start.1 = ((bf16[24,4,2176]{2,1,0:T(4,128)(2,1)}), bf16[24,4,2176]{2,1,0:T(4,128)(2,1)S(1)}, u32[]{:S(2)}, u32[]{:S(2)}) async-start(bf16[24,4,2176]{2,1,0:T(4,128)(2,1)} %visual_attention.1), calls=%async_computation.1 | async-start | bytes 835584 | tf_op jit(solution)/shard_map/all_to_all | solution.py:25
  29.3 8.4 %copy-start.2 = (s32[128]{0:T(128)S(1)}, s32[128]{0:T(128)}, u32[]{:S(2)}) copy-start(s32[128]{0:T(128)} %get-tuple-element.11.slot_hbm) | copy-start | bytes 1540
  37.7 2.5 %copy-start.1 = (s32[8,12]{1,0:T(8,128)S(1)}, s32[8,12]{1,0:T(8,128)}, u32[]{:S(2)}) copy-start(s32[8,12]{1,0:T(8,128)} %param.13) | copy-start | bytes 1156

commit v7 on v6

--- a/solution.py
+++ b/solution.py
@@ -12,7 +12,7 @@
 EPSILON = 1e-06
 LANES = 128
 FLOOR = -1e30
-RUNS = 2
+RUNS = 1
 ORDERS = {8: (5, 7, 4, 1, 3, 6, 2, 0)}
 FAR_BYTES = 36 << 20
 

time: 40.6 us -> 40.7 us (level)
  no operation moved by 1% of the time
where the time goes in v7:
time: 40.7 us; the launch traced here: 40.3 us
  Pallas kernels  22.3 us (55%)
  starting transfers between devices  13.6 us (33%)
  waiting for transfers between devices  3.69 us (9%)
  other arithmetic  0.57 us (1%)
    all_to_all x2, starting transfers between devices, exchange(): lax.all_to_all(slots, 'dp', split_axis=0, concat_axis=0, tiled=True, axis...  13.5 us
    pallas_call x1, Pallas kernels, project(): pl.pallas_call(kernel, in_specs=[hbm, hbm], out_specs=[pl.BlockSpec(memor...  8.67 us
    pallas_call x1, Pallas kernels, cached_attention(): pl.pallas_call(kernel, grid_spec=pltpu.PrefetchScalarGridSpec(num_scalar_...  6.3 us
    pallas_call x1, Pallas kernels, visual_attention(): pl.pallas_call(kernel, in_specs=[anywhere, vmem, vmem, anywhere], out_spe...  2.75 us
    pallas_call x1, Pallas kernels, merge(): pl.pallas_call(kernel, in_specs=[anywhere, pl.BlockSpec(memory_space=pltp...  2.5 us
    pallas_call x1, Pallas kernels, pack_queries(): pl.pallas_call(kernel, in_specs=[pl.BlockSpec(memory_space=pl.ANY), pl.Bl...  2.13 us
    all_to_all x2, waiting for transfers between devices, exchange(): lax.all_to_all(slots, 'dp', split_axis=0, concat_axis=0, tiled=True, axis...  2.07 us
    ppermute x1, waiting for transfers between devices, shards(): from_partner = lax.ppermute(for_partner, 'tensor', [(0, 1), (1, 0)])  1.62 us
  transfers between devices with their start and end apart: 3, of which 2 were waited for; matrix products, arithmetic and copies ran while one was open for 1% of the time, Pallas kernels for 37%

profile of v7, /device:TPU:0, one launch (start us, length us, event | category | flops | bytes accessed | tf_op | source)
XLA Modules:
  0.0 40.3 jit_solution(14802343061844713608)
XLA Ops:
  0.0 0.0 copy-start
  0.0 0.0 copy-start.4
  0.0 0.0 copy-start.3
  0.0 2.1 %pack_queries.1 = (bf16[24,4,2048]{2,1,0:T(4,128)(2,1)}, s32[128]{0:T(128)}) custom-call(s32[96]{0:T(128)} %owner_hbm.1, bf16[24,4,2048]{2,1,0:T(4,128)(2,1)} %q_ref.1), custom_call_target="tpu_custom_call" | custom-call | tf_op jit(solution)/shard_map/pack_queries/pallas_call | solution.py:96
  2.1 8.4 %all-to-all-start = ((bf16[24,4,2048]{2,1,0:T(4,128)(2,1)}), bf16[24,4,2048]{2,1,0:T(4,128)(2,1)S(1)}, u32[]{:S(2)}, u32[]{:S(2)}) async-start(bf16[24,4,2048]{2,1,0:T(4,128)(2,1)} %get-tuple-element.13), calls=%async_computation | async-start | bytes 786432 | tf_op jit(solution)/shard_map/all_to_all | solution.py:25
  10.6 8.7 %project.1 = (bf16[480,640]{1,0:T(8,128)(2,1)}, bf16[29491,640]{1,0:T(8,128)(2,1)}) custom-call(bf16[480,4096]{1,0:T(8,128)(2,1)} %token_hbm, bf16[4096,2,512]{2,1,0:T(2,128)(2,1)} %bitcast.3), custom_call_target="tpu_custom_call" | custom-call | flops 1048576 | bytes 65536 | tf_op jit(solution)/shard_map/project/pallas_call | solution.py:193
  19.2 0.1 collective-permute-start
  19.3 0.0 copy-done.3
  19.3 0.1 and_select_fusion.1
  19.4 0.2 convert_reduce_fusion
  19.6 0.0 copy-done.4
  19.6 0.1 select_reduce_fusion.1
  19.7 0.0 copy-done
  19.7 0.1 select_reduce_fusion
  19.8 0.1 pad_add_fusion.place_hbm
  19.9 1.6 %collective-permute-done.received_ref = bf16[480,640]{1,0:T(8,128)(2,1)S(1)} collective-permute-done((bf16[480,640]{1,0:T(8,128)(2,1)}, bf16[480,640]{1,0:T(8,128)(2,1)S(1)}, u32[]{:S(2)}, u32[]{:S(2)}) %collective-permute-start) | collective-permute-done | bytes 614432 | tf_op jit(solution)/shard_map/ppermute | solution.py:533
  21.5 0.0 all-to-all-done.q_ref
  21.5 2.8 %visual_attention.1 = bf16[24,4,2176]{2,1,0:T(4,128)(2,1)} custom-call(s32[48]{0:T(128)S(1)} %pad_add_fusion.place_hbm, bf16[24,4,2048]{2,1,0:T(4,128)(2,1)S(1)} %all-to-all-done.q_ref, bf16[480,640]{1,0:T(8,128)(2,1)S(1)} %collective-permute-done.received_ref, bf16[29491,640]{1,0:T(8,128)(2,1)} %get-tuple-element.16.ours_hbm), custom_call_target="tpu_custom_call" | custom-call | tf_op jit(solution)/shard_map/visual_attention/pallas_call | solution.py:417
  24.3 5.1 %all-to-all-start.1 = ((bf16[24,4,2176]{2,1,0:T(4,128)(2,1)}), bf16[24,4,2176]{2,1,0:T(4,128)(2,1)S(1)}, u32[]{:S(2)}, u32[]{:S(2)}) async-start(bf16[24,4,2176]{2,1,0:T(4,128)(2,1)} %visual_attention.1), calls=%async_computation.1 | async-start | bytes 835584 | tf_op jit(solution)/shard_map/all_to_all | solution.py:25
  29.4 0.0 copy-start.2
  29.4 6.3 %cached_attention.1.cached_hbm = f32[4336,2176]{1,0:T(8,128)} custom-call(s32[24]{0:T(128)} %length_ref.1, bf16[24,4,2048]{2,1,0:T(4,128)(2,1)} %q_ref.1, bf16[24,128,256]{2,1,0:T(8,128)(2,1)} %k_ref.1, bf16[24,128,256]{2,1,0:T(8,128)(2,1)} %v_ref.1, bf16[24,4,256]{2,1,0:T(4,128)(2,1)} %sk_ref.1, bf16[24,4,256]{2,1,0:T(4,128)(2,1)} %sv_ref.1), custom_call_target="tpu_custom_call" | custom-call | flops 1048576 | bytes 65536 | tf_op jit(solution)/shard_map/cached_attention/pallas_call | solution.py:280
  35.7 2.1 %all-to-all-done.1.returned_ref = bf16[24,4,2176]{2,1,0:T(4,128)(2,1)S(1)} async-done(((bf16[24,4,2176]{2,1,0:T(4,128)(2,1)}), bf16[24,4,2176]{2,1,0:T(4,128)(2,1)S(1)}, u32[]{:S(2)}, u32[]{:S(2)}) %all-to-all-start.1) | async-done | bytes 417824 | tf_op jit(solution)/shard_map/all_to_all | solution.py:25
  37.8 0.0 copy-done.2
  37.8 0.0 copy-start.1
  37.8 2.5 %merge.1 = bf16[24,4,2048]{2,1,0:T(4,128)(2,1)} custom-call(s32[128]{0:T(128)S(1)} %copy-done.2, bf16[24,4,2176]{2,1,0:T(4,128)(2,1)S(1)} %all-to-all-done.1.returned_ref, f32[4336,2176]{1,0:T(8,128)} %cached_attention.1.cached_hbm), custom_call_target="tpu_custom_call" | custom-call | tf_op jit(solution)/shard_map/merge/pallas_call | solution.py:494
  40.3 0.0 copy-done.1
  (3 shorter events, 0.0 us)
Async XLA Ops:
  0.0 19.7 %copy-start = (s32[8,12]{1,0:T(8,128)S(1)}, s32[8,12]{1,0:T(8,128)}, u32[]{:S(2)}) copy-start(s32[8,12]{1,0:T(8,128)} %param.13) | copy-start | bytes 1156
  0.0 19.6 %copy-start.4 = (s32[8]{0:T(128)S(1)}, s32[8]{0:T(128)}, u32[]{:S(2)}) copy-start(s32[8]{0:T(128)} %constant.46.clone) | copy-start | bytes 100
  0.0 19.3 %copy-start.3 = (s32[96]{0:T(128)S(1)}, s32[96]{0:T(128)}, u32[]{:S(2)}) copy-start(s32[96]{0:T(128)} %owner_hbm.1) | copy-start | bytes 1156
  2.1 19.4 %all-to-all-start = ((bf16[24,4,2048]{2,1,0:T(4,128)(2,1)}), bf16[24,4,2048]{2,1,0:T(4,128)(2,1)S(1)}, u32[]{:S(2)}, u32[]{:S(2)}) async-start(bf16[24,4,2048]{2,1,0:T(4,128)(2,1)} %get-tuple-element.13), calls=%async_computation | async-start | bytes 786432 | tf_op jit(solution)/shard_map/all_to_all | solution.py:25
  19.2 2.3 %collective-permute-start = (bf16[480,640]{1,0:T(8,128)(2,1)}, bf16[480,640]{1,0:T(8,128)(2,1)S(1)}, u32[]{:S(2)}, u32[]{:S(2)}) collective-permute-start(bf16[480,640]{1,0:T(8,128)(2,1)} %get-tuple-element.15), channel_id=1, source_target_pairs={{0,1},{1,0},{2,3},{3,2},{4,5},{5,4},{6,7},{7,6},{8,9},{9,8},{10,11... | collective-permute-start | bytes 1843208 | tf_op jit(solution)/shard_map/ppermute | solution.py:533
  24.3 13.5 %all-to-all-start.1 = ((bf16[24,4,2176]{2,1,0:T(4,128)(2,1)}), bf16[24,4,2176]{2,1,0:T(4,128)(2,1)S(1)}, u32[]{:S(2)}, u32[]{:S(2)}) async-start(bf16[24,4,2176]{2,1,0:T(4,128)(2,1)} %visual_attention.1), calls=%async_computation.1 | async-start | bytes 835584 | tf_op jit(solution)/shard_map/all_to_all | solution.py:25
  29.4 8.4 %copy-start.2 = (s32[128]{0:T(128)S(1)}, s32[128]{0:T(128)}, u32[]{:S(2)}) copy-start(s32[128]{0:T(128)} %get-tuple-element.11.slot_hbm) | copy-start | bytes 1540
  37.8 2.5 %copy-start.1 = (s32[8,12]{1,0:T(8,128)S(1)}, s32[8,12]{1,0:T(8,128)}, u32[]{:S(2)}) copy-start(s32[8,12]{1,0:T(8,128)} %param.13) | copy-start | bytes 1156
